TPU v7x, 32 devices: a whole 2x2x4 slice. The times are simulated.
32 devices in a mesh: dp: 16 (over z, y, x), sub: 2 (over core).
Axes of the slice: x: 2, y: 2, z: 4, core: 2. Of those that a mesh axis runs over, the one named last changes fastest.
Arguments:
- item_ids: int32 [16, 512], replicated, may hold values from 0 to 25087, as said below
- lengths: int32 [16], replicated, may hold values from 1 to 512, 6963 in all
- home_row: int32 [25088], replicated, may hold values from 0 to 25087, as said below
- log_freq: float32 [25088], replicated, may hold values from -3 to 0
- item_table: float32 [25088, 256], P('dp'), may hold values from -0.72 to 0.72
- table_first: float32 [25088, 256], P('dp')
- table_second: float32 [25088, 256], P('dp')
- pos_table: float32 [512, 256], P(None, ('dp', 'sub')), may hold values from -0.72 to 0.72
- pos_first: float32 [512, 256], P(None, ('dp', 'sub'))
- pos_second: float32 [512, 256], P(None, ('dp', 'sub'))
- qkv_weight: float32 [256, 768], P(None, ('dp', 'sub')), may hold values from -0.375 to 0.375
- qkv_first: float32 [256, 768], P(None, ('dp', 'sub'))
- qkv_second: float32 [256, 768], P(None, ('dp', 'sub'))
- merge_weight: float32 [256, 256], P(None, ('dp', 'sub')), may hold values from -1.5 to 1.5
- merge_first: float32 [256, 256], P(None, ('dp', 'sub'))
- merge_second: float32 [256, 256], P(None, ('dp', 'sub'))
- widen_weight: float32 [256, 1024], P(None, ('dp', 'sub')), may hold values from -0.375 to 0.375
- widen_first: float32 [256, 1024], P(None, ('dp', 'sub'))
- widen_second: float32 [256, 1024], P(None, ('dp', 'sub'))
- narrow_weight: float32 [1024, 256], P(None, ('dp', 'sub')), may hold values from -0.1875 to 0.1875
- narrow_first: float32 [1024, 256], P(None, ('dp', 'sub'))
- narrow_second: float32 [1024, 256], P(None, ('dp', 'sub'))
- norm_gains: float32 [3, 256], P(None, ('dp', 'sub')), may hold values from 0.5 to 1.5
- gains_first: float32 [3, 256], P(None, ('dp', 'sub'))
- gains_second: float32 [3, 256], P(None, ('dp', 'sub'))
Outputs:
- loss_sum: float32 [], replicated
- event_count: float32 [], replicated
- grad_norm: float32 [], replicated
- table_next: float32 [25088, 256], P('dp')
- table_first_next: float32 [25088, 256], P('dp')
- table_second_next: float32 [25088, 256], P('dp')
- pos_next: float32 [512, 256], P(None, ('dp', 'sub'))
- pos_first_next: float32 [512, 256], P(None, ('dp', 'sub'))
- pos_second_next: float32 [512, 256], P(None, ('dp', 'sub'))
- qkv_next: float32 [256, 768], P(None, ('dp', 'sub'))
- qkv_first_next: float32 [256, 768], P(None, ('dp', 'sub'))
- qkv_second_next: float32 [256, 768], P(None, ('dp', 'sub'))
- merge_next: float32 [256, 256], P(None, ('dp', 'sub'))
- merge_first_next: float32 [256, 256], P(None, ('dp', 'sub'))
- merge_second_next: float32 [256, 256], P(None, ('dp', 'sub'))
- widen_next: float32 [256, 1024], P(None, ('dp', 'sub'))
- widen_first_next: float32 [256, 1024], P(None, ('dp', 'sub'))
- widen_second_next: float32 [256, 1024], P(None, ('dp', 'sub'))
- narrow_next: float32 [1024, 256], P(None, ('dp', 'sub'))
- narrow_first_next: float32 [1024, 256], P(None, ('dp', 'sub'))
- narrow_second_next: float32 [1024, 256], P(None, ('dp', 'sub'))
- gains_next: float32 [3, 256], P(None, ('dp', 'sub'))
- gains_first_next: float32 [3, 256], P(None, ('dp', 'sub'))
- gains_second_next: float32 [3, 256], P(None, ('dp', 'sub'))
Inputs may be any that keep to these rules, and one draw needn't show every extreme that they name: `item_ids`: of the slots of one device (the histories of one index of dp, the positions of one index of sub), at most 32 hold items whose table rows one index of dp holds, and some index of dp holds exactly 32 of them. A permutation: item i lives in row home_row[i] of item_table, held by the index home_row[i] // 1568 of dp. History h has its events in its first lengths[h] slots; some history fills all 512.
All inputs are finite; a program needn't handle non-finite values.
Results may differ from a plain program's by a relative error of at most 0.012.
The roundings to bfloat16 on the way count: a program that leaves them out, or rounds other values in their place, can miss the bound.
Values may be sent and summed in bfloat16 or wider, within the bound.
A program may use at most 384 MiB of HBM per device.

v0:
```python
import math

import jax
import jax.numpy as jnp
from jax import lax
from jax.sharding import PartitionSpec as P

HEADS = 8
STEP = 10


norm_eps = 1e-06
beta_one = 0.9
beta_two = 0.999
adam_eps = 1e-08
decay_rate = 0.01
learn_rate = 0.1
gain_rate = 0.5
clip_limit = 0.01
big_negative = -1e30
block_cols = 4096


def dot_plain(left_mat, right_mat):
    return jnp.dot(left_mat, right_mat, preferred_element_type=jnp.float32)


def dot_left_t(left_mat, right_mat):
    return lax.dot_general(
        left_mat, right_mat, (((0,), (0,)), ((), ())), preferred_element_type=jnp.float32
    )


def dot_right_t(left_mat, right_mat):
    return lax.dot_general(
        left_mat, right_mat, (((1,), (1,)), ((), ())), preferred_element_type=jnp.float32
    )


def rms_forward(values, gain_row):
    inverse = lax.rsqrt(jnp.mean(values * values, axis=-1, keepdims=True) + norm_eps)
    return (values * inverse * gain_row, inverse)


def rms_backward(upstream, values, inverse, gain_row):
    unit_vals = values * inverse
    gain_grad = jnp.sum(upstream * unit_vals, axis=0)
    scaled = upstream * gain_row
    inner_mean = jnp.mean(scaled * unit_vals, axis=-1, keepdims=True)
    return (inverse * (scaled - unit_vals * inner_mean), gain_grad)


def head_scores(queries, keys_all, allowed):
    scaling = queries.shape[-1] ** (-0.5)
    plain_scores = (
        jnp.einsum("bqhe,bkhe->bhqk", queries, keys_all, preferred_element_type=jnp.float32)
        * scaling
    )
    return jnp.where(allowed, plain_scores, big_negative)


def target_of(indices, slice_len, tokens_dev):
    within = indices % slice_len
    return jnp.where(within + 1 < slice_len, indices + 1, indices - within + tokens_dev)


def logits_for(user_rows, cand_rows, corr_rows, valid_rows):
    logits = dot_right_t(user_rows, cand_rows) - corr_rows[None, :]
    return jnp.where(valid_rows[None, :], logits, big_negative)


def coefficient(logits, log_total, weights, columns, targets):
    hits = (columns[None, :] == targets[:, None]).astype(jnp.float32)
    return (weights[:, None] * (jnp.exp(logits - log_total[:, None]) - hits)).astype(jnp.bfloat16)


def block_forward(resid_zero, dense_w, allowed, hist_local):
    qkv_full, merge_full, widen_full, narrow_full, gains_full = dense_w
    gain_float = gains_full.astype(jnp.float32)
    tokens_dev, model_width = resid_zero.shape
    normed_one, inverse_one = rms_forward(resid_zero, gain_float[0])
    input_one = normed_one.astype(jnp.bfloat16)
    qkv_parts = (
        dot_plain(input_one, qkv_full)
        .astype(jnp.bfloat16)
        .reshape(hist_local, -1, 3, HEADS, model_width // HEADS)
    )
    queries = qkv_parts[:, :, 0]
    keys_all, values_all = (
        lax.all_gather(qkv_parts[:, :, 1], "sub", axis=1, tiled=True),
        lax.all_gather(qkv_parts[:, :, 2], "sub", axis=1, tiled=True),
    )
    scores = head_scores(queries, keys_all, allowed)
    row_peak = jnp.max(scores, axis=-1, keepdims=True)
    expo_vals = jnp.exp(scores - row_peak)
    row_total = jnp.sum(expo_vals, axis=-1, keepdims=True)
    log_total = row_peak + jnp.log(row_total)
    attn_prob = (expo_vals / row_total).astype(jnp.bfloat16)
    attended = jnp.einsum(
        "bhqk,bkhe->bqhe", attn_prob, values_all, preferred_element_type=jnp.float32
    )
    attended = attended.astype(jnp.bfloat16).reshape(tokens_dev, model_width)
    resid_one = resid_zero + dot_plain(attended, merge_full)
    normed_two, inverse_two = rms_forward(resid_one, gain_float[1])
    input_two = normed_two.astype(jnp.bfloat16)
    hidden_pre = dot_plain(input_two, widen_full)
    hidden_act = jax.nn.gelu(hidden_pre).astype(jnp.bfloat16)
    resid_two = resid_one + dot_plain(hidden_act, narrow_full)
    normed_three, inverse_three = rms_forward(resid_two, gain_float[2])
    kept = (
        resid_zero,
        inverse_one,
        input_one,
        queries,
        keys_all,
        values_all,
        log_total,
        attended,
        resid_one,
        inverse_two,
        input_two,
        hidden_pre,
        hidden_act,
        resid_two,
        inverse_three,
    )
    return (normed_three.astype(jnp.bfloat16), kept)


def block_backward(user_grad, kept, dense_w, allowed):
    (
        resid_zero,
        inverse_one,
        input_one,
        queries,
        keys_all,
        values_all,
        log_total,
        attended,
        resid_one,
        inverse_two,
        input_two,
        hidden_pre,
        hidden_act,
        resid_two,
        inverse_three,
    ) = kept
    qkv_full, merge_full, widen_full, narrow_full, gains_full = dense_w
    gain_float = gains_full.astype(jnp.float32)
    tokens_dev, model_width = resid_zero.shape
    head_dim = queries.shape[-1]
    grad_two, gain_three = rms_backward(user_grad, resid_two, inverse_three, gain_float[2])
    branch_two = grad_two.astype(jnp.bfloat16)
    narrow_grad = dot_left_t(hidden_act, branch_two)
    hidden_grad = dot_right_t(branch_two, narrow_full)
    pre_grad = jax.vjp(jax.nn.gelu, hidden_pre)[1](hidden_grad)[0].astype(jnp.bfloat16)
    widen_grad = dot_left_t(input_two, pre_grad)
    from_two, gain_two = rms_backward(
        dot_right_t(pre_grad, widen_full), resid_one, inverse_two, gain_float[1]
    )
    grad_one = grad_two + from_two
    branch_one = grad_one.astype(jnp.bfloat16)
    merge_grad = dot_left_t(attended, branch_one)
    mixed_grad = dot_right_t(branch_one, merge_full).astype(jnp.bfloat16).reshape(queries.shape)
    scores = head_scores(queries, keys_all, allowed)
    attn_prob = jnp.exp(scores - log_total)
    prob_grad = jnp.einsum(
        "bqhe,bkhe->bhqk", mixed_grad, values_all, preferred_element_type=jnp.float32
    )
    score_grad = attn_prob * (prob_grad - jnp.sum(attn_prob * prob_grad, axis=-1, keepdims=True))
    score_grad = score_grad.astype(jnp.bfloat16)
    scaling = head_dim ** (-0.5)
    query_grad = (
        jnp.einsum("bhqk,bkhe->bqhe", score_grad, keys_all, preferred_element_type=jnp.float32)
        * scaling
    )
    keys_grad = (
        jnp.einsum("bhqk,bqhe->bkhe", score_grad, queries, preferred_element_type=jnp.float32)
        * scaling
    )
    values_grad = jnp.einsum(
        "bhqk,bqhe->bkhe",
        attn_prob.astype(jnp.bfloat16),
        mixed_grad,
        preferred_element_type=jnp.float32,
    )
    key_own, value_own = (
        lax.psum_scatter(
            keys_grad.astype(jnp.bfloat16), "sub", scatter_dimension=1, tiled=True
        ).astype(jnp.float32),
        lax.psum_scatter(
            values_grad.astype(jnp.bfloat16), "sub", scatter_dimension=1, tiled=True
        ).astype(jnp.float32),
    )
    qkv_grad = (
        jnp.stack([query_grad, key_own, value_own], axis=2)
        .astype(jnp.bfloat16)
        .reshape(tokens_dev, 3 * model_width)
    )
    qkv_wgrad = dot_left_t(input_one, qkv_grad)
    from_one, gain_one = rms_backward(
        dot_right_t(qkv_grad, qkv_full), resid_zero, inverse_one, gain_float[0]
    )
    gain_grads = jnp.stack([gain_one, gain_two, gain_three])
    return (grad_one + from_one, (qkv_wgrad, merge_grad, widen_grad, narrow_grad, gain_grads))


def adamw(weight, moment_one, moment_two, gradient, rate):
    moment_one = beta_one * moment_one + (1.0 - beta_one) * gradient
    moment_two = beta_two * moment_two + (1.0 - beta_two) * gradient * gradient
    fix_one = 1.0 - beta_one**STEP
    fix_two = 1.0 - beta_two**STEP
    update = (
        moment_one / fix_one / (jnp.sqrt(moment_two / fix_two) + adam_eps) + decay_rate * weight
    )
    return (weight - rate * update, moment_one, moment_two)


def body(
    item_ids,
    lengths,
    home_row,
    log_freq,
    item_table,
    table_first,
    table_second,
    pos_table,
    pos_first,
    pos_second,
    qkv_weight,
    qkv_first,
    qkv_second,
    merge_weight,
    merge_first,
    merge_second,
    widen_weight,
    widen_first,
    widen_second,
    narrow_weight,
    narrow_first,
    narrow_second,
    norm_gains,
    gains_first,
    gains_second,
):
    dp_count = lax.axis_size("dp")
    sub_count = lax.axis_size("sub")
    dp_index = lax.axis_index("dp")
    sub_index = lax.axis_index("sub")
    rows_dev, model_width = item_table.shape
    hist_local = item_ids.shape[0] // dp_count
    seq_len = item_ids.shape[1]
    slice_len = seq_len // sub_count
    tokens_dev = hist_local * slice_len
    capacity = max(2, (2 * tokens_dev + dp_count - 1) // dp_count)
    all_tokens = dp_count * sub_count * tokens_dev
    pos_full, qkv_full, merge_full, widen_full, narrow_full, gains_full = (
        lax.all_gather(pos_table.astype(jnp.bfloat16), ("dp", "sub"), axis=1, tiled=True),
        lax.all_gather(qkv_weight.astype(jnp.bfloat16), ("dp", "sub"), axis=1, tiled=True),
        lax.all_gather(merge_weight.astype(jnp.bfloat16), ("dp", "sub"), axis=1, tiled=True),
        lax.all_gather(widen_weight.astype(jnp.bfloat16), ("dp", "sub"), axis=1, tiled=True),
        lax.all_gather(narrow_weight.astype(jnp.bfloat16), ("dp", "sub"), axis=1, tiled=True),
        lax.all_gather(norm_gains.astype(jnp.bfloat16), ("dp", "sub"), axis=1, tiled=True),
    )
    dense_w = (qkv_full, merge_full, widen_full, narrow_full, gains_full)
    own_items = lax.dynamic_slice(
        item_ids, (dp_index * hist_local, sub_index * slice_len), (hist_local, slice_len)
    ).reshape(tokens_dev)
    stored_at = home_row[own_items]
    owner_dev = stored_at // rows_dev
    local_row = stored_at % rows_dev
    owner_hot = (owner_dev[:, None] == jnp.arange(dp_count, dtype=jnp.int32)[None, :]).astype(
        jnp.int32
    )
    owner_rank = jnp.sum(jnp.cumsum(owner_hot, axis=0) * owner_hot, axis=1) - 1
    slot_index = owner_dev * capacity + owner_rank
    request = (
        jnp.zeros((dp_count * capacity,), jnp.int32)
        .at[slot_index]
        .set(local_row)
        .reshape(dp_count, capacity)
    )
    arrived = lax.all_to_all(request, "dp", split_axis=0, concat_axis=0, tiled=True)
    found_rows = item_table[arrived].astype(jnp.bfloat16)
    arrived_rows = lax.all_to_all(found_rows, "dp", split_axis=0, concat_axis=0, tiled=True)
    embedded = arrived_rows.reshape(dp_count * capacity, model_width)[slot_index]
    pos_rows = lax.dynamic_slice_in_dim(pos_full, sub_index * slice_len, slice_len, 0).astype(
        jnp.float32
    )
    resid_zero = (
        embedded.astype(jnp.float32).reshape(hist_local, slice_len, model_width) + pos_rows[None]
    ).reshape(tokens_dev, model_width)
    query_pos = sub_index * slice_len + jnp.arange(slice_len)
    allowed = jnp.arange(seq_len)[None, :] <= query_pos[:, None]
    user_vecs, kept = block_forward(resid_zero, dense_w, allowed, hist_local)
    candidates = lax.all_gather(embedded, ("dp", "sub"), axis=0, tiled=True)
    layout = (dp_count, hist_local, sub_count, slice_len)

    def by_device(values):
        return values.reshape(layout).transpose(0, 2, 1, 3).reshape(all_tokens)

    all_items = by_device(item_ids)
    all_pos = by_device(
        jnp.broadcast_to(jnp.arange(seq_len, dtype=jnp.int32)[None, :], item_ids.shape)
    )
    all_len = by_device(jnp.broadcast_to(lengths[:, None], item_ids.shape))
    valid_all = (all_pos >= 1) & (all_pos < all_len)
    correction = log_freq[all_items]
    base_index = (dp_index * sub_count + sub_index) * tokens_dev
    own_index = base_index + jnp.arange(tokens_dev)
    own_pos = lax.dynamic_slice_in_dim(all_pos, base_index, tokens_dev)
    own_len = lax.dynamic_slice_in_dim(all_len, base_index, tokens_dev)
    event_count = jnp.sum(lengths - 1).astype(jnp.float32)
    valid_rows = (own_pos + 1 < own_len).astype(jnp.float32)
    row_weight = valid_rows / event_count
    targets = target_of(own_index, slice_len, tokens_dev)
    col_block = min(block_cols, all_tokens)
    starts = jnp.arange(all_tokens // col_block) * col_block

    def block_logits(block_start):
        cand_rows = lax.dynamic_slice_in_dim(candidates, block_start, col_block, 0)
        corr_rows = lax.dynamic_slice_in_dim(correction, block_start, col_block)
        valid_cols = lax.dynamic_slice_in_dim(valid_all, block_start, col_block)
        return (
            cand_rows,
            logits_for(user_vecs, cand_rows, corr_rows, valid_cols),
            block_start + jnp.arange(col_block),
        )

    def forward_block(running, block_start):
        row_peak, row_total, target_logit = running
        cand_rows, logits, columns = block_logits(block_start)
        new_peak = jnp.maximum(row_peak, jnp.max(logits, axis=1))
        row_total = row_total * jnp.exp(row_peak - new_peak) + jnp.sum(
            jnp.exp(logits - new_peak[:, None]), axis=1
        )
        target_logit = target_logit + jnp.sum(
            jnp.where(columns[None, :] == targets[:, None], logits, 0.0), axis=1
        )
        return ((new_peak, row_total, target_logit), None)

    start_state = (
        jnp.full((tokens_dev,), big_negative, jnp.float32),
        jnp.zeros((tokens_dev,), jnp.float32),
        jnp.zeros((tokens_dev,), jnp.float32),
    )
    (row_peak, row_total, target_logit), _ = lax.scan(forward_block, start_state, starts)
    log_total = row_peak + jnp.log(row_total)
    loss_local = jnp.sum(valid_rows * (log_total - target_logit))

    def user_block(running, block_start):
        cand_rows, logits, columns = block_logits(block_start)
        coeffs = coefficient(logits, log_total, row_weight, columns, targets)
        return (running + dot_plain(coeffs, cand_rows), None)

    user_grad, _ = lax.scan(user_block, jnp.zeros((tokens_dev, model_width), jnp.float32), starts)
    step_rows = math.gcd(tokens_dev * lax.axis_size(("dp", "sub")), max(block_cols, tokens_dev))

    def one_block(offset):
        cand_rows = lax.dynamic_slice_in_dim(candidates, offset, step_rows, 0)
        corr_rows = lax.dynamic_slice_in_dim(correction, offset, step_rows)
        valid_cols = lax.dynamic_slice_in_dim(valid_all, offset, step_rows)
        logits = logits_for(user_vecs, cand_rows, corr_rows, valid_cols)
        coeffs = coefficient(logits, log_total, row_weight, offset + jnp.arange(step_rows), targets)
        return dot_left_t(coeffs, user_vecs)

    pieces = lax.map(
        one_block, jnp.arange(tokens_dev * lax.axis_size(("dp", "sub")) // step_rows) * step_rows
    )
    cand_grad = lax.psum_scatter(
        pieces.reshape(tokens_dev * lax.axis_size(("dp", "sub")), model_width),
        ("dp", "sub"),
        scatter_dimension=0,
        tiled=True,
    )
    resid_grad, weight_grads = block_backward(user_grad, kept, dense_w, allowed)
    qkv_wgrad, merge_grad, widen_grad, narrow_grad, gain_grads = weight_grads
    emb_grad = resid_grad + cand_grad
    pos_rows_grad = jnp.sum(resid_grad.reshape(hist_local, slice_len, model_width), axis=0)
    pos_grad = lax.dynamic_update_slice_in_dim(
        jnp.zeros((seq_len, model_width), jnp.float32), pos_rows_grad, sub_index * slice_len, 0
    )
    outgoing = (
        jnp.zeros((dp_count * capacity, model_width), jnp.float32).at[slot_index].set(emb_grad)
    )
    incoming = lax.all_to_all(
        outgoing.reshape(dp_count, capacity, model_width),
        "dp",
        split_axis=0,
        concat_axis=0,
        tiled=True,
    )
    incoming_rows = incoming.reshape(-1, model_width)
    arrived_flat = arrived.reshape(-1)
    plane_grad = jnp.zeros((rows_dev, model_width), jnp.float32).at[arrived_flat].add(incoming_rows)
    table_grad = lax.psum(plane_grad, "sub")
    shard_grads = (
        lax.psum_scatter(pos_grad, ("dp", "sub"), scatter_dimension=1, tiled=True),
        lax.psum_scatter(qkv_wgrad, ("dp", "sub"), scatter_dimension=1, tiled=True),
        lax.psum_scatter(merge_grad, ("dp", "sub"), scatter_dimension=1, tiled=True),
        lax.psum_scatter(widen_grad, ("dp", "sub"), scatter_dimension=1, tiled=True),
        lax.psum_scatter(narrow_grad, ("dp", "sub"), scatter_dimension=1, tiled=True),
        lax.psum_scatter(gain_grads, ("dp", "sub"), scatter_dimension=1, tiled=True),
    )
    square_part = sum((jnp.sum(gradient * gradient) for gradient in shard_grads))
    square_part = square_part + jnp.where(sub_index == 0, jnp.sum(table_grad * table_grad), 0.0)
    loss_sum, square_sum = lax.psum((loss_local, square_part), ("dp", "sub"))
    grad_norm = jnp.sqrt(square_sum)
    factor = jnp.minimum(1.0, clip_limit / grad_norm)
    masters = (
        item_table,
        pos_table,
        qkv_weight,
        merge_weight,
        widen_weight,
        narrow_weight,
        norm_gains,
    )
    firsts = (
        table_first,
        pos_first,
        qkv_first,
        merge_first,
        widen_first,
        narrow_first,
        gains_first,
    )
    seconds = (
        table_second,
        pos_second,
        qkv_second,
        merge_second,
        widen_second,
        narrow_second,
        gains_second,
    )
    rates = (learn_rate,) * 6 + (gain_rate,)
    all_grads = (table_grad,) + tuple(shard_grads)
    results = [loss_sum, event_count, grad_norm]
    for weight, moment_one, moment_two, gradient, rate in zip(
        masters, firsts, seconds, all_grads, rates
    ):
        results.extend(adamw(weight, moment_one, moment_two, gradient * factor, rate))
    return tuple(results)


def solution(mesh):
    placed = (
        P(),
        P(),
        P(),
        P(),
        P("dp", None),
        P("dp", None),
        P("dp", None),
        P(None, ("dp", "sub")),
        P(None, ("dp", "sub")),
        P(None, ("dp", "sub")),
        P(None, ("dp", "sub")),
        P(None, ("dp", "sub")),
        P(None, ("dp", "sub")),
        P(None, ("dp", "sub")),
        P(None, ("dp", "sub")),
        P(None, ("dp", "sub")),
        P(None, ("dp", "sub")),
        P(None, ("dp", "sub")),
        P(None, ("dp", "sub")),
        P(None, ("dp", "sub")),
        P(None, ("dp", "sub")),
        P(None, ("dp", "sub")),
        P(None, ("dp", "sub")),
        P(None, ("dp", "sub")),
        P(None, ("dp", "sub")),
    )
    return jax.shard_map(
        body,
        mesh=mesh,
        in_specs=placed,
        out_specs=(
            P(),
            P(),
            P(),
            P("dp", None),
            P("dp", None),
            P("dp", None),
            P(None, ("dp", "sub")),
            P(None, ("dp", "sub")),
            P(None, ("dp", "sub")),
            P(None, ("dp", "sub")),
            P(None, ("dp", "sub")),
            P(None, ("dp", "sub")),
            P(None, ("dp", "sub")),
            P(None, ("dp", "sub")),
            P(None, ("dp", "sub")),
            P(None, ("dp", "sub")),
            P(None, ("dp", "sub")),
            P(None, ("dp", "sub")),
            P(None, ("dp", "sub")),
            P(None, ("dp", "sub")),
            P(None, ("dp", "sub")),
            P(None, ("dp", "sub")),
            P(None, ("dp", "sub")),
            P(None, ("dp", "sub")),
        ),
        check_vma=False,
    )
```

profile of v0, /device:TPU:0, one launch (start us, length us, event | category | flops | bytes accessed | tf_op | source)
XLA Modules:
  0.0 1285.7 jit_solution(6718208565403812438)
XLA Ops:
  8.1 2.1 gather_fusion
  11.3 1.4 scatter_custom_fusion
  12.8 15.4 %all_to_all.22 = s32[16,1,32]{2,1,0:T(1,128)S(1)} all-to-all(s32[16,1,32]{2,1,0:T(1,128)S(1)} %all_to_all.14), channel_id=1, replica_groups=mesh['dp'=16,'sub'=2] {'dp'}, dimensions={0} | all-to-all | bytes 4096 | tf_op jit(solution)/shard_map/all_to_all | solution.py:283
  28.8 3.6 gather_fusion.1
  32.4 3.5 all-to-all-start.1
  38.2 41.8 %all-gather.3 = bf16[32,8,3]{1,2,0:T(4,128)(2,1)S(1)} all-gather(bf16[1,8,3]{1,2,0:T(4,128)(2,1)S(1)} %convert_bitcast_fusion), channel_id=1, replica_groups=mesh['dp'=16,'sub'=2] {'dp','sub'}, dimensions={0}, use_global_device_ids=true | all-gather | bytes 1584 | tf_op jit(solution)/shard_map/all_gather | solution.py:263
  80.2 1.8 gather_fusion.2
  82.5 45.5 %gather_fusion.3 = f32[8192]{0:T(1024)S(1)} fusion(f32[25088]{0:T(1024)S(1)} %copy-done, s32[8192]{0:T(1024)S(1)} %broadcast_clamp_fusion), kind=kCustom, calls=%fused_computation.3 | custom fusion | bytes 98304 | tf_op jit(solution)/shard_map/gather | solution.py:308
  128.0 37.0 %all_gather.33 = bf16[256,256]{0,1:T(8,128)(2,1)S(1)} all-gather(bf16[256,8]{0,1:T(8,128)(2,1)S(1)} %convert_element_type.151), channel_id=1, replica_groups=mesh['dp'=16,'sub'=2] {'dp','sub'}, dimensions={1}, use_global_device_ids=true | all-gather | bytes 135168 | tf_op jit(solution)/shard_map/all_gather | solution.py:260
  166.2 38.7 %all_gather.28 = bf16[512,256]{0,1:T(8,128)(2,1)S(1)} all-gather(bf16[512,8]{0,1:T(8,128)(2,1)S(1)} %convert_element_type.140), channel_id=1, replica_groups=mesh['dp'=16,'sub'=2] {'dp','sub'}, dimensions={1}, use_global_device_ids=true | all-gather | bytes 270336 | tf_op jit(solution)/shard_map/all_gather | solution.py:258
  204.9 37.7 %all_gather.30 = bf16[256,768]{0,1:T(8,128)(2,1)S(1)} all-gather(bf16[256,24]{0,1:T(8,128)(2,1)S(1)} %convert_element_type.145), channel_id=1, replica_groups=mesh['dp'=16,'sub'=2] {'dp','sub'}, dimensions={1}, use_global_device_ids=true | all-gather | bytes 405504 | tf_op jit(solution)/shard_map/all_gather | solution.py:259
  243.3 39.5 %all_gather.35 = bf16[1024,256]{0,1:T(8,128)(2,1)S(1)} all-gather(bf16[1024,8]{0,1:T(8,128)(2,1)S(1)} %convert_element_type.155), channel_id=1, replica_groups=mesh['dp'=16,'sub'=2] {'dp','sub'}, dimensions={1}, use_global_device_ids=true | all-gather | bytes 540672 | tf_op jit(solution)/shard_map/all_gather | solution.py:262
  282.8 38.0 %all_gather.34 = bf16[256,1024]{0,1:T(8,128)(2,1)S(1)} all-gather(bf16[256,32]{0,1:T(8,128)(2,1)S(1)} %convert_element_type.153), channel_id=1, replica_groups=mesh['dp'=16,'sub'=2] {'dp','sub'}, dimensions={1}, use_global_device_ids=true | all-gather | bytes 540672 | tf_op jit(solution)/shard_map/all_gather | solution.py:261
  321.7 2.0 all-gather.1
  323.7 2.2 all-gather.2
  328.0 1.4 fusion.65
  332.1 18.7 %while.38 = (s32[]{:T(128)}, f32[256]{0:T(256)S(1)}, f32[256]{0:T(256)S(1)}, f32[256]{0:T(256)S(1)}, s32[2]{0:T(128)}, /*index=5*/pred[8192]{0:T(1024)(128)(4,1)...) while((s32[]{:T(128)}, f32[256]{0:T(256)S(1)}, ...), condition=%wide.region_13.14_spmd.clone, body=%wide.region_9.13_spmd.clone.sunk | while | flops 545269760 | bytes 10730706 | solution.py:347
  336.2 3.3 fusion.160
  339.5 1.9 fusion.162
  345.5 3.4 fusion.160
  348.9 1.9 fusion.162
  351.4 18.7 %while.39 = (s32[]{:T(128)}, f32[256,256]{1,0:T(8,128)S(1)}, f32[256]{0:T(256)S(1)}, s32[2]{0:T(128)}, pred[8192]{0:T(1024)(128)(4,1)S(1)}, /*index=5*/bf16[8192...) while((s32[]{:T(128)}, f32[256,256]{1,0:T(8,128)S(1)}, ...), condition=%wide.region_18.19_spmd.clone, body=%wide.region_17.18_spmd.clone.sunk | while | flops 1082270208 | bytes 4949708 | solution.py:356
  355.5 5.3 fusion.166
  364.8 5.3 fusion.166
  372.3 2.4 fusion.73
  376.1 1.5 fusion.60
  377.7 5.9 multiply_reduce_fusion
  383.9 4.1 multiply_convert_fusion
  388.0 2.1 fusion.63
  390.1 21.9 %while.37 = (s32[]{:T(128)}, f32[2,4096,256]{2,1,0:T(8,128)}, f32[256]{0:T(256)}, s32[2]{0:T(128)}, pred[8192]{0:T(1024)(128)(4,1)S(1)}, /*index=5*/bf16[8192,25...) while((s32[]{:T(128)}, f32[2,4096,256]{2,1,0:T(8,128)}, ...), condition=%wide.region_41.42_spmd.clone, body=%wide.region_40.41_spmd.clone.sunk | while | flops 1082139136 | bytes 6652107 | solution.py:367
  395.9 5.2 fusion.158
  406.9 5.2 fusion.158
  412.0 8.9 copy.142
  425.3 2.9 fusion.87
  428.2 1.4 fusion.106
  430.7 136.4 %reduce-scatter.24.cloned.1.call-done = f32[256,256]{0,1:T(8,128)} async-done(((f32[8192,256]{0,1:T(8,128)}), f32[256,256]{0,1:T(8,128)}) %reduce-scatter.24.cloned.1.call-update) | async-done | bytes 262160 | tf_op jit(solution)/shard_map/reduce_scatter | solution.py:370
  567.1 1.8 fusion.116
  570.2 1.9 copy.138
  572.1 2.6 scatter_custom_fusion.1
  574.7 4.2 all-to-all-start.2
  580.3 11.8 all-to-all-done.2
  592.1 5.1 scatter_custom_fusion.2
  597.9 39.0 %all-reduce = f32[3,256]{1,0:T(4,128)S(1)} all-reduce(f32[3,256]{1,0:T(4,128)S(1)} %pad_maximum_fusion.1), channel_id=12, replica_groups=mesh['dp'=16,'sub'=2] {'dp','sub'}, use_global_device_ids=true, to_apply=%region_38.39.clone | all-reduce | flops 768 | bytes 6144
  637.6 61.7 %reduce-scatter.18.cloned.1.call-done = f32[256,8]{0,1:T(8,128)} async-done(((f32[256,256]{0,1:T(8,128)}), f32[256,8]{0,1:T(8,128)}) %reduce-scatter.18.cloned.1.call-update) | async-done | bytes 8208 | tf_op jit(solution)/shard_map/reduce_scatter | solution.py:400
  699.3 1.3 multiply_reduce_fusion.15
  700.6 95.9 %reduce-scatter.16.cloned.1.call-done = f32[256,24]{0,1:T(8,128)} async-done(((f32[256,768]{0,1:T(8,128)}), f32[256,24]{0,1:T(8,128)}) %reduce-scatter.16.cloned.1.call-update) | async-done | bytes 24592 | tf_op jit(solution)/shard_map/reduce_scatter | solution.py:399
  796.5 1.3 multiply_reduce_fusion.14
  797.8 135.4 %reduce-scatter.22.cloned.1.call-done = f32[1024,8]{0,1:T(8,128)} async-done(((f32[1024,256]{0,1:T(8,128)}), f32[1024,8]{0,1:T(8,128)}) %reduce-scatter.22.cloned.1.call-update) | async-done | bytes 32784 | tf_op jit(solution)/shard_map/reduce_scatter | solution.py:402
  933.3 1.4 multiply_reduce_fusion.12
  934.6 132.2 %reduce-scatter.20.cloned.1.call-done = f32[256,32]{0,1:T(8,128)} async-done(((f32[256,1024]{0,1:T(8,128)}), f32[256,32]{0,1:T(8,128)}) %reduce-scatter.20.cloned.1.call-update) | async-done | bytes 32784 | tf_op jit(solution)/shard_map/reduce_scatter | solution.py:401
  1066.9 1.4 multiply_reduce_fusion.13
  1068.2 130.9 %reduce-scatter.26.cloned.1.call-done = f32[8,512]{1,0:T(8,128)} async-done(((f32[256,512]{1,0:T(8,128)}), f32[8,512]{1,0:T(8,128)}) %reduce-scatter.26.cloned.1.call-update) | async-done | bytes 16400
  1199.1 1.6 copy.144
  1200.7 1.6 multiply_reduce_fusion.5
  1206.2 12.1 all-reduce.4.cloned.1.call-done
  1218.3 2.4 multiply_reduce_fusion.1
  1221.4 41.1 %all-reduce.1 = (f32[]{:T(128)}, f32[]{:T(128)}) all-reduce(f32[]{:T(128)} %get-tuple-element.545, f32[]{:T(128)S(6)} %add.463), channel_id=1, replica_groups=mesh['dp'=16,'sub'=2] {'dp','sub'}, use_global_device_ids=true, to_apply=%region_15.16 | all-reduce | flops 2 | bytes 16 | tf_op jit(solution)/shard_map/psum | solution.py:407
  1263.3 1.4 multiply_subtract_fusion.6
  1264.6 1.4 multiply_subtract_fusion.5
  1266.0 1.4 multiply_subtract_fusion.4
  1267.4 1.4 multiply_subtract_fusion.3
  1268.8 1.4 multiply_subtract_fusion.1
  1270.2 1.4 multiply_subtract_fusion.2
  1271.7 5.0 multiply_subtract_fusion
  (256 shorter events, 41.7 us)
Async XLA Ops:
  7.2 75.3 %copy-start = (f32[25088]{0:T(1024)S(1)}, f32[25088]{0:T(1024)}, u32[]{:S(2)}) copy-start(f32[25088]{0:T(1024)} %param.34) | copy-start | bytes 301060
  7.2 72.9 %copy-start.29 = (s32[16,512]{1,0:T(8,128)S(1)}, s32[16,512]{1,0:T(8,128)}, u32[]{:S(2)}) copy-start(s32[16,512]{1,0:T(8,128)} %param.31) | copy-start | bytes 98308
  7.2 74.8 %copy-start.54 = (s32[16]{0:T(128)S(1)}, s32[16]{0:T(128)}, u32[]{:S(2)}) copy-start(s32[16]{0:T(128)} %param.32) | copy-start | bytes 196
  7.2 30.8 %copy-start.33 = (f32[256,8]{0,1:T(8,128)S(1)}, f32[256,8]{0,1:T(8,128)}, u32[]{:S(2)}) copy-start(f32[256,8]{0,1:T(8,128)} %param.44) | copy-start | bytes 24580
  7.2 30.8 %copy-start.25 = (f32[512,8]{0,1:T(8,128)S(1)}, f32[512,8]{0,1:T(8,128)}, u32[]{:S(2)}) copy-start(f32[512,8]{0,1:T(8,128)} %param.38) | copy-start | bytes 49156
  7.3 30.8 %copy-start.21 = (f32[256,24]{0,1:T(8,128)S(1)}, f32[256,24]{0,1:T(8,128)}, u32[]{:S(2)}) copy-start(f32[256,24]{0,1:T(8,128)} %param.41) | copy-start | bytes 73732
  7.3 30.8 %copy-start.17 = (f32[256,32]{0,1:T(8,128)S(1)}, f32[256,32]{0,1:T(8,128)}, u32[]{:S(2)}) copy-start(f32[256,32]{0,1:T(8,128)} %param.47) | copy-start | bytes 98308
  7.3 30.9 %copy-start.15 = (f32[1024,8]{0,1:T(8,128)S(1)}, f32[1024,8]{0,1:T(8,128)}, u32[]{:S(2)}) copy-start(f32[1024,8]{0,1:T(8,128)} %param.50) | copy-start | bytes 98308
  7.3 30.9 %copy-start.48 = (f32[3,8]{1,0:T(4,128)S(1)}, f32[3,8]{1,0:T(4,128)}, u32[]{:S(2)}) copy-start(f32[3,8]{1,0:T(4,128)} %param.53) | copy-start | bytes 292
  11.3 116.8 %copy-start.50 = (s32[256,1]{0,1:T(1,128)}, s32[256,1]{0,1:T(1,128)S(1)}, u32[]{:S(2)}) copy-start(s32[256,1]{0,1:T(1,128)S(1)} %compare_select_fusion.12) | copy-start | bytes 3076
  32.4 47.7 %all-to-all-start.1 = ((bf16[16,32,256]{2,1,0:T(8,128)(2,1)}), bf16[16,32,256]{2,1,0:T(8,128)(2,1)S(1)}, u32[]{:S(2)}, u32[]{:S(2)}) async-start(bf16[16,32,256]{2,1,0:T(8,128)(2,1)} %bitcast.9), calls=%async_computation.1 | async-start | bytes 524288 | tf_op jit(solution)/shard_map/all_to_all | solution.py:285
  36.0 296.0 %all-gather.6.cloned.1.call-start = ((), (), s32[]{:S(2)}) async-start(), calls=%async_computation.19 | async-start | bytes 4325376 | tf_op jit(solution)/shard_map/all_gather | solution.py:296
  82.0 340.8 %reduce-scatter.14.cloned.1.call-start = ((), (), s32[]{:S(2)}) async-start(), calls=%async_computation.12 | async-start | bytes 393216 | tf_op jit(solution)/shard_map/reduce_scatter | solution.py:191
  82.5 238.4 %copy-start.10 = (bf16[256,256]{1,0:T(8,128)(2,1)S(1)}, bf16[256,256]{1,0:T(8,128)(2,1)}, u32[]{:S(2)}) copy-start(bf16[256,256]{1,0:T(8,128)(2,1)} %gather_fusion.2) | copy-start | bytes 393220
  242.5 78.5 %copy-start.8 = (bf16[256,768]{0,1:T(8,128)(2,1)}, bf16[256,768]{0,1:T(8,128)(2,1)S(1)}, u32[]{:S(2)}) copy-start(bf16[256,768]{0,1:T(8,128)(2,1)S(1)} %all_gather.30) | copy-start | bytes 1179652
  243.1 83.7 %copy-start.46 = (f32[1,256]{1,0:T(1,128)}, f32[1,256]{1,0:T(1,128)S(1)}, u32[]{:S(2)}) copy-start(f32[1,256]{1,0:T(1,128)S(1)} %get-tuple-element.558) | copy-start | bytes 3076
  243.2 86.6 %copy-start.38 = (f32[1,256]{1,0:T(1,128)}, f32[1,256]{1,0:T(1,128)S(1)}, u32[]{:S(2)}) copy-start(f32[1,256]{1,0:T(1,128)S(1)} %get-tuple-element.557) | copy-start | bytes 3076
  282.8 47.3 %copy-start.13 = (bf16[1024,256]{0,1:T(8,128)(2,1)}, bf16[1024,256]{0,1:T(8,128)(2,1)S(1)}, u32[]{:S(2)}) copy-start(bf16[1024,256]{0,1:T(8,128)(2,1)S(1)} %all_gather.35) | copy-start | bytes 1572868
  321.7 6.4 copy-start.4
  326.8 2.6 copy-start.1
  329.4 2.3 copy-start.41
  329.4 2.6 copy-start.27
  329.5 2.6 copy-start.28
  329.7 2.3 copy-start.35
  330.2 1.0 copy-start.12
  332.0 45.7 %copy-start.20 = (f32[8,256]{1,0:T(8,128)}, f32[8,256]{1,0:T(8,128)S(1)}, u32[]{:S(2)}) copy-start(f32[8,256]{1,0:T(8,128)S(1)} %log_add_fusion) | copy-start | bytes 24580
  332.0 18.7 %copy-start.51 = (pred[256]{0:T(512)(128)(4,1)S(1)}, pred[256]{0:T(512)(128)(4,1)}, u32[]{:S(2)}) copy-start(pred[256]{0:T(512)(128)(4,1)} %get-tuple-element.544) | copy-start | bytes 772
  332.1 19.4 %copy-start.14 = (f32[256,256]{1,0:T(8,128)S(1)}, f32[256,256]{1,0:T(8,128)}, u32[]{:S(2)}) copy-start(f32[256,256]{1,0:T(8,128)} %custom-call.3) | copy-start | bytes 786436
  332.1 19.3 %copy-start.53 = (f32[256]{0:T(256)S(1)}, f32[256]{0:T(256)}, u32[]{:S(2)}) copy-start(f32[256]{0:T(256)} %get-tuple-element.845) | copy-start | bytes 3076
  351.4 20.8 %copy-start.42 = (f32[1,256]{1,0:T(1,128)S(1)}, f32[1,256]{1,0:T(1,128)}, u32[]{:S(2)}) copy-start(f32[1,256]{1,0:T(1,128)} %get-tuple-element.556) | copy-start | bytes 3076
  370.1 0.6 copy-start.19
  371.4 3.3 copy-start.36
  371.5 3.3 copy-start.39
  372.3 3.5 copy-start.11
  372.3 3.8 copy-start.2
  374.8 8.9 copy-start.5
  383.6 39.2 %reduce-scatter.12.cloned.1.call-start = ((), (), s32[]{:S(2)}) async-start(), calls=%async_computation.11 | async-start | bytes 393216 | tf_op jit(solution)/shard_map/reduce_scatter | solution.py:188
  390.1 177.0 %reduce-scatter.24.cloned.1.call-start = ((), (), s32[]{:S(2)}) async-start(), calls=%async_computation.17 | async-start | bytes 8650752 | tf_op jit(solution)/shard_map/reduce_scatter | solution.py:370
  420.9 2.9 copy-start.45
  421.0 2.9 copy-start.47
  421.0 278.3 %reduce-scatter.18.cloned.1.call-start = ((), (), s32[]{:S(2)}) async-start(), calls=%async_computation.14 | async-start | bytes 270336 | tf_op jit(solution)/shard_map/reduce_scatter | solution.py:400
  422.0 6.2 copy-start.37
  422.0 6.2 copy-start.40
  422.0 374.5 %reduce-scatter.16.cloned.1.call-start = ((), (), s32[]{:S(2)}) async-start(), calls=%async_computation.13 | async-start | bytes 811008 | tf_op jit(solution)/shard_map/reduce_scatter | solution.py:399
  422.8 5.5 copy-start.6
  425.2 4.5 copy-start.9
  425.2 508.1 %reduce-scatter.22.cloned.1.call-start = ((), (), s32[]{:S(2)}) async-start(), calls=%async_computation.16 | async-start | bytes 1081344 | tf_op jit(solution)/shard_map/reduce_scatter | solution.py:402
  428.1 638.7 %reduce-scatter.20.cloned.1.call-start = ((), (), s32[]{:S(2)}) async-start(), calls=%async_computation.15 | async-start | bytes 1081344 | tf_op jit(solution)/shard_map/reduce_scatter | solution.py:401
  429.6 149.9 %copy-start.24 = (s32[16,1,32]{2,1,0:T(1,128)S(1)}, s32[16,1,32]{2,1,0:T(1,128)}, u32[]{:S(2)}) copy-start(s32[16,1,32]{2,1,0:T(1,128)} %copy-done.23) | copy-start | bytes 6148
  429.7 769.5 %reduce-scatter.26.cloned.1.call-start = ((), (), s32[]{:S(2)}) async-start(), calls=%async_computation.20 | async-start | bytes 540672
  570.1 693.2 %copy-start.49 = (f32[3,8]{1,0:T(4,128)S(1)}, f32[3,8]{1,0:T(4,128)}, u32[]{:S(2)}) copy-start(f32[3,8]{1,0:T(4,128)} %param.53) | copy-start | bytes 292
  570.1 694.6 %copy-start.34 = (f32[256,8]{0,1:T(8,128)S(1)}, f32[256,8]{0,1:T(8,128)}, u32[]{:S(2)}) copy-start(f32[256,8]{0,1:T(8,128)} %param.44) | copy-start | bytes 24580
  570.1 695.9 %copy-start.26 = (f32[512,8]{0,1:T(8,128)S(1)}, f32[512,8]{0,1:T(8,128)}, u32[]{:S(2)}) copy-start(f32[512,8]{0,1:T(8,128)} %param.38) | copy-start | bytes 49156
  570.1 697.3 %copy-start.22 = (f32[256,24]{0,1:T(8,128)S(1)}, f32[256,24]{0,1:T(8,128)}, u32[]{:S(2)}) copy-start(f32[256,24]{0,1:T(8,128)} %param.41) | copy-start | bytes 73732
  570.1 698.7 %copy-start.16 = (f32[1024,8]{0,1:T(8,128)S(1)}, f32[1024,8]{0,1:T(8,128)}, u32[]{:S(2)}) copy-start(f32[1024,8]{0,1:T(8,128)} %param.50) | copy-start | bytes 98308
  570.1 698.7 %copy-start.30 = (f32[1024,8]{0,1:T(8,128)S(1)}, f32[1024,8]{0,1:T(8,128)}, u32[]{:S(2)}) copy-start(f32[1024,8]{0,1:T(8,128)} %param.51) | copy-start | bytes 98308
  570.1 698.7 %copy-start.31 = (f32[1024,8]{0,1:T(8,128)S(1)}, f32[1024,8]{0,1:T(8,128)}, u32[]{:S(2)}) copy-start(f32[1024,8]{0,1:T(8,128)} %param.52) | copy-start | bytes 98308
  570.1 700.1 %copy-start.18 = (f32[256,32]{0,1:T(8,128)S(1)}, f32[256,32]{0,1:T(8,128)}, u32[]{:S(2)}) copy-start(f32[256,32]{0,1:T(8,128)} %param.47) | copy-start | bytes 98308
  570.1 700.1 %copy-start.32 = (f32[256,32]{0,1:T(8,128)S(1)}, f32[256,32]{0,1:T(8,128)}, u32[]{:S(2)}) copy-start(f32[256,32]{0,1:T(8,128)} %param.48) | copy-start | bytes 98308
  570.2 701.5 %copy-start.3 = (f32[1568,256]{1,0:T(8,128)S(1)}, f32[1568,256]{1,0:T(8,128)}, u32[]{:S(2)}) copy-start(f32[1568,256]{1,0:T(8,128)} %param.35) | copy-start | bytes 4816900
  570.2 701.5 %copy-start.7 = (f32[1568,256]{1,0:T(8,128)S(1)}, f32[1568,256]{1,0:T(8,128)}, u32[]{:S(2)}) copy-start(f32[1568,256]{1,0:T(8,128)} %param.36) | copy-start | bytes 4816900
  574.7 17.4 %all-to-all-start.2 = ((f32[16,32,256]{2,1,0:T(8,128)}), f32[16,32,256]{2,1,0:T(8,128)}, u32[]{:S(2)}, u32[]{:S(2)}) async-start(f32[16,32,256]{2,1,0:T(8,128)} %bitcast.43), calls=%async_computation.9 | async-start | bytes 1048576 | tf_op jit(solution)/shard_map/all_to_all | solution.py:386
  579.0 639.4 %all-reduce.4.cloned.1.call-start = ((), (), s32[]{:S(2)}) async-start(), calls=%async_computation.18 | async-start | bytes 3211264 | tf_op jit(solution)/shard_map/psum | solution.py:396
  580.3 685.7 %copy-start.43 = (f32[512,8]{0,1:T(8,128)S(1)}, f32[512,8]{0,1:T(8,128)}, u32[]{:S(2)}) copy-start(f32[512,8]{0,1:T(8,128)} %param.39) | copy-start | bytes 49156
  (3 other events, 1.8 us)
Sparse Core Ops, SparseCore 0:
  82.1 58.2 all-gather.5
  383.8 5.1 reduce-scatter.13
  391.2 8.8 reduce-scatter.11
  421.1 145.9 reduce-scatter.23
  569.1 130.0 reduce-scatter.17
  705.0 91.3 reduce-scatter.15
  799.4 133.8 reduce-scatter.21
  936.1 130.7 reduce-scatter.19
  1069.2 129.9 reduce-scatter.25
  1201.9 16.3 all-reduce.3
where the time goes:
time: 1290 us
  waiting for transfers between devices  717 us (56%)
  blocking collectives  332 us (26%)
  local copies, waits for them, and re-layouts  85.9 us (7%)
  other arithmetic  54.2 us (4%)
  matrix products  52.8 us (4%)
  between operations  23.5 us (2%)
    reduce_scatter x1, waiting for transfers between devices, body(): lax.psum_scatter(pieces.reshape(tokens_dev * lax.axis_size(('dp', 'sub'))...  136 us
    reduce_scatter x1, waiting for transfers between devices, body(): lax.psum_scatter(narrow_grad, ('dp', 'sub'), scatter_dimension=1, tiled=T...  135 us
    reduce_scatter x1, waiting for transfers between devices, body(): lax.psum_scatter(widen_grad, ('dp', 'sub'), scatter_dimension=1, tiled=True)  132 us
    unnamed x11, waiting for transfers between devices  131 us
    reduce_scatter x1, waiting for transfers between devices, body(): lax.psum_scatter(qkv_wgrad, ('dp', 'sub'), scatter_dimension=1, tiled=True)  95.9 us
    reduce_scatter x1, waiting for transfers between devices, body(): lax.psum_scatter(merge_grad, ('dp', 'sub'), scatter_dimension=1, tiled=True)  61.7 us
    gather x1, local copies, waits for them, and re-layouts, body(): correction = log_freq[all_items]  45.5 us
    all_gather x1, blocking collectives, body(): lax.all_gather(norm_gains.astype(jnp.bfloat16), ('dp', 'sub'), axis=1, ti...  41.8 us
  transfers between devices with their start and end apart: 12, of which 8 were waited for; matrix products, arithmetic and copies ran while one was open for 9% of the time, Pallas kernels for 0%

commit v1 on v0

--- a/solution.py
+++ b/solution.py
@@ -1,8 +1,12 @@
+import functools
 import math
+import types
 
 import jax
 import jax.numpy as jnp
 from jax import lax
+from jax.experimental import pallas as pl
+from jax.experimental.pallas import tpu as pltpu
 from jax.sharding import PartitionSpec as P
 
 HEADS = 8
@@ -444,6 +448,1057 @@
     return tuple(results)
 
 
+MESH_ID = pl.DeviceIdType.MESH
+FF_CHUNK = 256
+
+
+def dot_nn(left, right):
+    return lax.dot_general(
+        left, right, (((1,), (0,)), ((), ())), preferred_element_type=jnp.float32
+    )
+
+
+def dot_nt(left, right):
+    return lax.dot_general(
+        left, right, (((1,), (1,)), ((), ())), preferred_element_type=jnp.float32
+    )
+
+
+def dot_tn(left, right):
+    return lax.dot_general(
+        left, right, (((0,), (0,)), ((), ())), preferred_element_type=jnp.float32
+    )
+
+
+def low(values):
+    return values.astype(jnp.bfloat16)
+
+
+def wide(values):
+    return values.astype(jnp.float32)
+
+
+def iota_of(shape, axis):
+    return lax.broadcasted_iota(jnp.int32, shape, axis)
+
+
+def flip(index, bits):
+    total = 0
+    for power in (1, 2, 4, 8):
+        a = lax.rem(lax.div(index, power), 2)
+        b = (bits // power) % 2 if isinstance(bits, int) else lax.rem(lax.div(bits, power), 2)
+        total = total + power * (a + b - 2 * a * b)
+    return total
+
+
+def arrival_order(levels):
+    above = range(1, levels)
+    return (
+        [(0, 0), (0, 1), (0, 2)]
+        + [(level, 0) for level in above]
+        + [(0, 3)]
+        + [(level, corner) for level in above for corner in (1, 2)]
+        + [(level, 3) for level in above]
+    )
+
+
+class Place:
+    def __init__(self, chips):
+        self.chips = chips
+        self.chip = lax.axis_index("dp")
+        self.core = lax.axis_index("sub")
+        self.level = lax.div(self.chip, 4)
+        self.corner = lax.rem(self.chip, 4)
+        self.near_x = self.level * 4 + flip(self.corner, 1)
+        self.near_y = self.level * 4 + flip(self.corner, 2)
+
+    def way(self, step):
+        order = arrival_order(self.chips // 4)
+        if isinstance(step, int):
+            return order[step]
+        return tuple(
+            sum(jnp.where(step == i, place[axis], 0) for i, place in enumerate(order) if place[axis])
+            for axis in range(2)
+        )
+
+    def relative(self, step):
+        level, corner = self.way(step)
+        return flip(self.level, level) * 4 + flip(self.corner, corner)
+
+
+def remote(src, dst, send, recv, chip, core):
+    return pltpu.make_async_remote_copy(
+        src_ref=src,
+        dst_ref=dst,
+        send_sem=send,
+        recv_sem=recv,
+        device_id=(chip, core),
+        device_id_type=MESH_ID,
+    )
+
+
+class Gather:
+    def __init__(self, place, buf, send, recv):
+        self.place, self.buf, self.send, self.recv = place, buf, send, recv
+        self.levels = place.chips // 4
+        self.passed = 1
+
+    def copy(self, block, sem, chip, core):
+        return remote(
+            self.buf.at[block], self.buf.at[block], self.send.at[sem], self.recv.at[block], chip, core
+        )
+
+    def block(self, step, other=False):
+        place = self.place
+        return place.relative(step) * 2 + (1 - place.core if other else place.core)
+
+    def send_on(self, step, action):
+        place = self.place
+        block = self.block(step)
+        action(self.copy(block, step * 3, place.chip, 1 - place.core))
+
+        def to_x():
+            action(self.copy(block, step * 3 + 1, place.near_x, place.core))
+
+        def to_y():
+            action(self.copy(block, step * 3 + 2, place.near_y, place.core))
+
+        level, corner = place.way(step)
+        if corner == 0:
+            to_x()
+            to_y()
+        elif corner == 1 and level % 2 == 0:
+            to_y()
+        elif corner == 2 and level % 2 == 1:
+            to_x()
+
+    def along_z(self, action):
+        place = self.place
+        block = self.block(0)
+        for step in range(1, self.levels):
+            chip = flip(place.level, step) * 4 + place.corner
+            action(self.copy(block, place.chips * 3 + step - 1, chip, place.core))
+
+    def start(self):
+        self.along_z(lambda copy: copy.start())
+        self.send_on(0, lambda copy: copy.start())
+
+    def arrived(self, step, other=False):
+        place = self.place
+        self.copy(self.block(step, other), 0, place.chip, 1 - place.core).wait_recv()
+
+    def pass_on(self, step):
+        self.arrived(step)
+        self.send_on(step, lambda copy: copy.start())
+
+    def advance(self, count):
+        for _ in range(min(count, self.place.chips - self.passed)):
+            self.pass_on(self.passed)
+            self.passed += 1
+
+    def complete(self):
+        self.advance(self.place.chips)
+        for step in range(self.place.chips):
+            self.arrived(step, other=True)
+
+    def sent(self):
+        self.along_z(lambda copy: copy.wait_send())
+        for step in range(self.place.chips):
+            self.send_on(step, lambda copy: copy.wait_send())
+
+    @staticmethod
+    def sends(chips):
+        return chips * 3 + chips // 4 - 1
+
+
+class Spread:
+    def __init__(self, place, buf, send, recv):
+        self.place, self.buf, self.send, self.recv = place, buf, send, recv
+        self.me, self.count = place.chip * 2 + place.core, place.chips * 2
+
+    def copy(self, other, at):
+        return remote(
+            self.buf.at[at], self.buf.at[at], self.send.at[other], self.recv.at[at],
+            lax.div(other, 2), lax.rem(other, 2),
+        )
+
+    def each(self, action):
+        def step(index, carry):
+            action(lax.rem(self.me + index, self.count))
+            return carry
+
+        lax.fori_loop(1, self.count, step, 0)
+
+    def start(self):
+        self.each(lambda other: self.copy(other, self.me).start())
+
+    def arrived(self):
+        self.each(lambda other: self.copy(other, other).wait_recv())
+
+    def sent(self):
+        self.each(lambda other: self.copy(other, self.me).wait_send())
+
+
+class Scatter:
+    def __init__(self, place, src, dst, send, recv):
+        self.place, self.src, self.dst, self.send, self.recv = place, src, dst, send, recv
+
+    def copy(self, to, at):
+        place = self.place
+        return remote(
+            self.src.at[to] if self.src is not None else self.dst.at[place.chip],
+            self.dst.at[at],
+            self.send.at[to],
+            self.recv.at[at],
+            to,
+            place.core,
+        )
+
+    def each(self, action):
+        place = self.place
+
+        def step(index, carry):
+            action(lax.rem(place.chip + index, place.chips))
+            return carry
+
+        lax.fori_loop(1, place.chips, step, 0)
+
+    def start(self):
+        self.each(lambda chip: self.copy(chip, self.place.chip).start())
+
+    def arrived(self):
+        self.each(lambda chip: self.copy(chip, chip).wait_recv())
+
+    def sent(self):
+        self.each(lambda chip: self.copy(chip, self.place.chip).wait_send())
+
+
+class Reduce:
+    def __init__(self, place, pack, pair, summed, plane, part, line, sems):
+        self.place, self.pack, self.pair, self.summed = place, pack, pair, summed
+        self.plane, self.part, self.line, self.sems = plane, part, line, sems
+        self.levels = place.chips // 4
+
+    def pair_copy(self):
+        place = self.place
+        return remote(
+            self.pack.at[1 - place.core], self.pair, self.sems.at[0], self.sems.at[1], place.chip, 1 - place.core
+        )
+
+    def plane_copy(self, way, coming=False):
+        place = self.place
+        corner = flip(place.corner, way)
+        return remote(
+            self.summed.at[corner], self.plane.at[corner if coming else place.corner],
+            self.sems.at[2 + way], self.sems.at[6 + way], place.level * 4 + corner, place.core,
+        )
+
+    def line_copy(self, way, coming=False):
+        place = self.place
+        level = flip(place.level, way)
+        return remote(
+            self.part.at[level], self.line.at[level if coming else place.level],
+            self.sems.at[10 + way], self.sems.at[10 + self.levels + way], level * 4 + place.corner, place.core,
+        )
+
+    def to_pair(self):
+        self.pair_copy().start()
+
+    def to_plane(self):
+        self.pair_copy().wait_recv()
+        place = self.place
+        for way in (3, 1, 2, 0):
+            corner = flip(place.corner, way)
+            for level in range(self.levels):
+                self.summed[corner, level] = low(
+                    wide(self.pack[place.core, corner, level]) + wide(self.pair[corner, level])
+                )
+            if way:
+                self.plane_copy(way).start()
+
+    def to_line(self):
+        place = self.place
+        corners = [flip(place.corner, way) for way in (1, 2, 3)]
+        for way in (1, 2, 3):
+            self.plane_copy(way, True).wait_recv()
+        for way in [*range(1, self.levels), 0]:
+            level = flip(place.level, way)
+            total = wide(self.summed[place.corner, level])
+            for corner in corners:
+                total = total + wide(self.plane[corner, level])
+            self.part[level] = low(total)
+            if way:
+                self.line_copy(way).start()
+
+    def total(self):
+        place = self.place
+        total = wide(self.part[place.level])
+        for way in range(1, self.levels):
+            self.line_copy(way, True).wait_recv()
+            total = total + wide(self.line[flip(place.level, way)])
+        return total
+
+    def sent(self):
+        self.pair_copy().wait_send()
+        for way in (1, 2, 3):
+            self.plane_copy(way).wait_send()
+        for way in range(1, self.levels):
+            self.line_copy(way).wait_send()
+
+
+def rms_apply(values, gain_row):
+    inverse = lax.rsqrt(jnp.mean(values * values, axis=-1, keepdims=True) + norm_eps)
+    return values * inverse * gain_row, inverse
+
+
+def rms_back(upstream, values, inverse, gain_row):
+    unit = values * inverse
+    gain_grad = jnp.sum(upstream * unit, axis=0, keepdims=True)
+    scaled = upstream * gain_row
+    inner = jnp.mean(scaled * unit, axis=-1, keepdims=True)
+    return inverse * (scaled - unit * inner), gain_grad
+
+
+GELU_A = math.sqrt(2.0 / math.pi)
+GELU_B = 0.044715
+
+
+def gelu_both(x):
+    square = x * x
+    curve = jnp.tanh(GELU_A * x * (1.0 + GELU_B * square))
+    half = 0.5 * (1.0 + curve)
+    slope = half + 0.5 * x * (1.0 - curve * curve) * (GELU_A * (1.0 + 3.0 * GELU_B * square))
+    return x * half, slope
+
+
+def pieces_of(values):
+    first = wide(low(values))
+    second = wide(low(values - first))
+    return first, second, values - first - second
+
+
+def step_kernel(sizes, *refs):
+    (chips, rows_dev, seq_len, width, hidden, capacity, half_slots, key_rows) = sizes
+    refs = list(refs)
+    names = list(dict(ENDS)) + list(scratch_of(sizes))
+    r = types.SimpleNamespace(**dict(zip(names, refs, strict=True)))
+    place = Place(chips)
+    chip, core = place.chip, place.core
+    me = chip * 2 + core
+    tokens = half_slots
+    wa, wb, cand_buf, user_buf = r.wa, r.wb, r.cand, r.user
+    gather_a = Gather(place, wa, r.wa_send, r.wa_recv)
+    gather_b = Gather(place, wb, r.wb_send, r.wb_recv)
+    gather_c = Gather(place, cand_buf, r.cand_send, r.cand_recv)
+    gather_u = Gather(place, user_buf, r.user_send, r.user_recv)
+    spread_corr = Spread(place, r.corr, r.corr_send, r.corr_recv)
+    spread_norm = Spread(place, r.norm, r.norm_send, r.norm_recv)
+    spread_sums = Spread(place, r.scalar_buf, r.scalar_send, r.scalar_recv)
+
+    barrier = pltpu.get_barrier_semaphore()
+
+    def greet(index, carry):
+        other = lax.rem(me + index, 2 * chips)
+        pl.semaphore_signal(
+            barrier, inc=1, device_id=(lax.div(other, 2), lax.rem(other, 2)), device_id_type=MESH_ID
+        )
+        return carry
+
+    lax.fori_loop(1, 2 * chips, greet, 0)
+
+    pos_t = r.pos[...]
+    wa[me] = low(
+        jnp.concatenate([r.qkv[...], r.gains[...], pos_t[:, :width], pos_t[:, width:]], axis=0)
+    )
+    narrow_t = r.narrow[...]
+    wb[me] = low(
+        jnp.concatenate(
+            [r.merge[...], r.widen[...]]
+            + [narrow_t[:, i * width : (i + 1) * width] for i in range(hidden // width)]
+            + [jnp.zeros((8, width), jnp.float32)],
+            axis=0,
+        )
+    )
+
+    low_table = r.low_table
+    low_table[pl.ds(0, rows_dev), :] = low(r.table[...])
+    pad_rows = low_table.shape[0] - rows_dev
+    low_table[pl.ds(rows_dev, pad_rows), :] = jnp.zeros((pad_rows, width), jnp.bfloat16)
+    keys = r.keys
+    keys[...] = jnp.zeros_like(keys)
+    home = r.home[...]
+    used = home.shape[0]
+    keys[pl.ds(0, used), pl.ds(0, 128)] = wide(lax.div(home, 256))
+    keys[pl.ds(0, used), pl.ds(128, 128)] = wide(lax.rem(home, 256))
+    home_look = low(jnp.transpose(keys[:, 0:256]))
+    ids_all = r.ids[:, pl.ds(pl.multiple_of(core * tokens, tokens), tokens)]
+    lane_of = iota_of((128, tokens), 0)
+    key_of = iota_of((key_rows, tokens), 0)
+
+    def look(table_t, ids_row, parts):
+        hot = low(wide(key_of == lax.div(ids_row, 128)))
+        picked = dot_nn(table_t, hot)
+        mask = lane_of == lax.rem(ids_row, 128)
+        return [
+            jnp.sum(jnp.where(mask, picked[128 * i : 128 * i + 128], 0.0), axis=0, keepdims=True)
+            for i in range(parts)
+        ]
+
+    home_rows = []
+    for d in range(chips):
+        top, bottom = look(home_look, ids_all[d : d + 1, :], 2)
+        home_rows.append(top * 256.0 + bottom)
+    home_all = jnp.concatenate(home_rows, axis=0)
+    r.home_all[...] = home_all
+
+    pl.semaphore_wait(barrier, 2 * chips - 1)
+    gather_a.start()
+
+    upper = low(wide(iota_of((tokens, tokens), 0) <= iota_of((tokens, tokens), 1)))
+    first_row = wide(chip * rows_dev)
+    local_all = home_all - first_row
+    owned = (local_all >= 0.0) & (local_all < float(rows_dev))
+    rank = dot_nn(low(wide(owned)), upper) - 1.0
+    slot_rank = wide(iota_of((capacity, tokens), 0))
+    wanted = []
+    for d in range(chips):
+        chosen = (rank[d : d + 1, :] == slot_rank) & owned[d : d + 1, :]
+        wanted.append(
+            jnp.sum(jnp.where(chosen, local_all[d : d + 1, :] + 1.0, 0.0), axis=1, keepdims=True) - 1.0
+        )
+    wanted = jnp.concatenate(wanted, axis=0)
+    asked = chips * capacity
+    lanes = low_table.shape[0]
+    hot_rows = low(wide(iota_of((asked, lanes), 1) == wanted.astype(jnp.int32)))
+    out_rows = low(dot_nn(hot_rows, low_table[...])).reshape(chips, capacity, width)
+    r.row_out[...] = out_rows
+    r.row_in[chip] = r.row_out[chip]
+    rows_there = Scatter(place, r.row_out, r.row_in, r.row_send, r.row_recv)
+    rows_there.start()
+    gather_b.start()
+    wanted_row = jnp.transpose(jnp.broadcast_to(wanted, (asked, 128)))[0:1, :]
+    r.asked[core] = wanted_row
+    asked_copy = remote(
+        r.asked.at[core], r.asked.at[core], r.asked_send, r.asked_recv, chip, 1 - core
+    )
+    asked_copy.start()
+
+    own_home = r.home_all[pl.ds(chip, 1), :]
+    owner_first = wide(iota_of((chips, tokens), 0) * rows_dev)
+    at_owner = (own_home >= owner_first) & (own_home < owner_first + float(rows_dev))
+    own_rank = dot_nn(low(wide(at_owner)), upper) - 1.0
+    spread = jnp.concatenate(
+        [
+            wide((own_rank[o : o + 1, :] == slot_rank) & at_owner[o : o + 1, :])
+            for o in range(chips)
+        ],
+        axis=0,
+    )
+    r.spread[...] = low(spread)
+
+    freq = r.freq[...]
+    for i, piece in enumerate(pieces_of(freq)):
+        keys[pl.ds(0, used), pl.ds(128 * i, 128)] = piece
+    freq_look = low(jnp.transpose(keys[...]))
+    own_ids = r.ids[pl.ds(chip, 1), pl.ds(pl.multiple_of(core * tokens, tokens), tokens)]
+    fa, fb, fc = look(freq_look, own_ids, 3)
+    own_length = r.lengths[chip]
+    row_pos = core * tokens + iota_of((1, tokens), 1)
+    is_cand = (row_pos >= 1) & (row_pos < own_length)
+    own_corr = jnp.where(is_cand, fa + fb + fc, -big_negative)
+    r.corr[me] = own_corr
+    spread_corr.start()
+
+    def turned(row):
+        return jnp.transpose(jnp.broadcast_to(row, (128, tokens)))[:, 0:1]
+
+    corr_col = turned(own_corr)
+    r.corr_col[...] = jnp.broadcast_to(corr_col, (tokens, 128))
+
+    total_events = jnp.float32(0.0)
+    for d in range(chips):
+        total_events = total_events + wide(r.lengths[d] - 1)
+    col_pos = core * tokens + iota_of((tokens, 1), 0)
+    is_event = col_pos + 1 < own_length
+
+    gather_a.advance(3)
+    rows_there.arrived()
+    embedded = low(dot_tn(r.spread[...], r.row_in[...].reshape(asked, width)))
+    cand_buf[me] = embedded
+    gather_c.start()
+    gather_a.advance(3)
+    gather_b.advance(3)
+    gather_a.complete()
+    qkv_w, pos_w, gain_w = r.qkv_w, r.pos_w, r.gain_w
+
+    def unpack_a(index, carry):
+        one, two = wide(wa[2 * index]), wide(wa[2 * index + 1])
+        qkv_w[pl.ds(pl.multiple_of(index * 48, 16), 48), :] = low(jnp.concatenate([one[0:24], two[0:24]], axis=0))
+        gain_w[pl.ds(pl.multiple_of(index * 16, 16), 16), :] = jnp.concatenate([one[24:32], two[24:32]], axis=0)[:, 0:128]
+        early = jnp.concatenate([one[32:40], two[32:40]], axis=0)
+        late = jnp.concatenate([one[40:48], two[40:48]], axis=0)
+        pos_w[pl.ds(pl.multiple_of(index * 16, 16), 16), :] = jnp.where(core == 0, early, late)
+        return carry
+
+    lax.fori_loop(0, chips, unpack_a, 0)
+    gain_rows = jnp.transpose(gain_w[...])[0:8, :]
+    r.gain_rows[...] = gain_rows
+    gain_one, gain_two, gain_three = (r.gain_rows[i : i + 1, :] for i in range(3))
+
+    resid_zero = wide(cand_buf[me]) + jnp.transpose(pos_w[...])
+    r.resid_zero[...] = resid_zero
+    normed, _ = rms_apply(resid_zero, gain_one)
+    r.input_one[...] = low(normed)
+    qkv_own = low(dot_nt(r.input_one[...], qkv_w[...]))
+    r.query[...] = qkv_own[:, 0:width]
+    kv = r.kv
+    kv[0] = qkv_own[:, width : 3 * width]
+    kv_copy = remote(kv.at[0], kv.at[1], r.kv_send, r.kv_recv, chip, 1 - core)
+    kv_copy.start()
+
+    gather_b.advance(3)
+    kv_copy.wait_recv()
+
+    head_dim = width // HEADS
+    scaling = head_dim ** (-0.5)
+    causal = iota_of((tokens, tokens), 1) <= iota_of((tokens, tokens), 0)
+    other_bias = jnp.where(core == 0, big_negative, 0.0)
+    head_lane = lax.div(iota_of((1, width), 1), head_dim)
+    prob = r.prob
+    mixed_sum = r.acc
+    mixed_sum[...] = jnp.zeros_like(mixed_sum)
+    zero_low = jnp.zeros((), jnp.bfloat16)
+
+    def of_head(values, head):
+        return jnp.where(head_lane == head, values, zero_low)
+
+    def attend(head):
+        query = of_head(r.query[...], head)
+        own = dot_nt(query, kv[0, :, 0:width]) * scaling
+        own = jnp.where(causal, own, big_negative)
+        other = dot_nt(query, kv[1, :, 0:width]) * scaling + other_bias
+        peak = jnp.maximum(
+            jnp.max(own, axis=-1, keepdims=True), jnp.max(other, axis=-1, keepdims=True)
+        )
+        own = jnp.exp(own - peak)
+        other = jnp.exp(other - peak)
+        total = jnp.sum(own, axis=-1, keepdims=True) + jnp.sum(other, axis=-1, keepdims=True)
+        share = 1.0 / total
+        own = own * share
+        other = other * share
+        prob[head, :, 0:tokens] = own
+        prob[head, :, tokens : 2 * tokens] = other
+        mixed_sum[...] += dot_nn(low(own), of_head(kv[0, :, width : 2 * width], head)) + dot_nn(
+            low(other), of_head(kv[1, :, width : 2 * width], head)
+        )
+
+    for head in range(HEADS):
+        attend(head)
+        if head % 2:
+            gather_b.advance(2)
+            gather_c.advance(1)
+    gather_b.complete()
+    merge_w, widen_w, narrow_w = r.merge_w, r.widen_w, r.narrow_w
+
+    def unpack_b(index, carry):
+        one, two = wide(wb[2 * index]), wide(wb[2 * index + 1])
+        at16 = pl.ds(pl.multiple_of(index * 16, 16), 16)
+        merge_w[at16, :] = low(jnp.concatenate([one[0:8], two[0:8]], axis=0))
+        widen_w[pl.ds(pl.multiple_of(index * 64, 16), 64), :] = low(jnp.concatenate([one[8:40], two[8:40]], axis=0))
+        for i in range(hidden // width):
+            top = 40 + 8 * i
+            narrow_w[at16, pl.ds(i * width, width)] = low(
+                jnp.concatenate([one[top : top + 8], two[top : top + 8]], axis=0)
+            )
+        return carry
+
+    lax.fori_loop(0, chips, unpack_b, 0)
+    r.attended[...] = low(mixed_sum[...])
+    resid_one = r.resid_zero[...] + dot_nt(r.attended[...], merge_w[...])
+    r.resid_one[...] = resid_one
+    normed, _ = rms_apply(resid_one, gain_two)
+    r.input_two[...] = low(normed)
+    r.resid_two[...] = resid_one
+    for i in range(hidden // FF_CHUNK):
+        part = slice(i * FF_CHUNK, (i + 1) * FF_CHUNK)
+        act, slope = gelu_both(dot_nt(r.input_two[...], widen_w[part, :]))
+        r.act[:, part] = low(act)
+        r.slope[:, part] = slope
+        gather_c.advance(1)
+    r.resid_two[...] += dot_nt(r.act[...], narrow_w[...])
+    normed, _ = rms_apply(r.resid_two[...], gain_three)
+    user_buf[me] = low(normed)
+    gather_u.start()
+
+    users = user_buf[me]
+    gather_c.advance(2)
+    gather_c.arrived(0, other=True)
+    spread_corr.arrived()
+    shifted = jnp.concatenate([wide(cand_buf[me])[1:, :], wide(cand_buf[chip * 2 + 1, pl.ds(0, 16), :])[0:1, :]], axis=0)
+    target_corr = jnp.concatenate([corr_col[1:, :], r.corr[chip * 2 + 1][:, 0:1]], axis=0)
+    target_logit = jnp.sum(wide(users) * shifted, axis=-1, keepdims=True) - target_corr
+    target_logit = jnp.where(is_event, target_logit, 0.0)
+    logit_buf, peaks, totals, acc = r.logit, r.peaks, r.totals, r.acc
+    totals[...] = jnp.zeros_like(totals)
+    acc[...] = jnp.zeros_like(acc)
+    both = 2 * tokens
+    group = chips // CHUNKS
+    chip_row = core * tokens + iota_of((tokens, both), 0)
+    chip_col = iota_of((tokens, both), 1)
+
+    def pair_rows(buf, there):
+        return buf[pl.ds(2 * there, 2)].reshape(both, width)
+
+    def pair_row(buf, there):
+        return jnp.concatenate([buf[2 * there], buf[2 * there + 1]], axis=1)
+
+    def fold(values, how):
+        parts = [values[:, i : i + 128] for i in range(0, values.shape[1], 128)]
+        return functools.reduce(how, parts)
+
+    peak = jnp.full((tokens, 1), big_negative, jnp.float32)
+    for chunk in range(CHUNKS):
+        gather_c.advance(group * (chunk + 1) - gather_c.passed)
+        peaks[...] = jnp.broadcast_to(peak, peaks.shape)
+
+        def logit_step(index, carry):
+            step = chunk * group + index
+
+            @pl.when(step > 0)
+            def _():
+                gather_c.arrived(step, other=True)
+
+            there = place.relative(step)
+            logits = dot_nt(users, pair_rows(cand_buf, there)) - pair_row(r.corr, there)
+            logit_buf[index] = logits
+            peaks[...] = jnp.maximum(peaks[...], fold(logits, jnp.maximum))
+            return carry
+
+        lax.fori_loop(0, group, logit_step, 0)
+        before, peak = peak, jnp.max(peaks[...], axis=-1, keepdims=True)
+        scale = jnp.exp(before - peak)
+        totals[...] *= scale
+        acc[...] *= scale
+        if chunk > 0:
+            gather_u.advance(2)
+
+        def expo_step(index, carry):
+            there = place.relative(chunk * group + index)
+            expo = jnp.exp(logit_buf[index] - peak)
+            totals[...] += fold(expo, jnp.add)
+            if chunk == 0:
+                expo = jnp.where((chip_col == chip_row + 1) & (index == 0), 0.0, expo)
+            acc[...] += dot_nn(low(expo), pair_rows(cand_buf, there))
+            return carry
+
+        lax.fori_loop(0, group, expo_step, 0)
+    total = jnp.sum(totals[...], axis=-1, keepdims=True)
+    log_total = peak + jnp.log(total)
+    loss_own = jnp.sum(jnp.where(is_event, log_total - target_logit, 0.0), axis=0, keepdims=True)
+    weight = jnp.where(is_event, 1.0 / total_events, 0.0)
+    target_coef = wide(low(weight * (jnp.exp(target_logit - log_total) - 1.0)))
+    user_grad = acc[...] * (weight / total) + target_coef * shifted
+    shift_col = jnp.where(is_event, log_total + jnp.log(total_events), -big_negative)
+    norm_buf = r.norm
+    norm_buf[me] = jnp.transpose(jnp.broadcast_to(shift_col, (tokens, 128)))[0:1, :]
+    spread_norm.start()
+    grad_two, gain_grad_three = rms_back(
+        user_grad, r.resid_two[...],
+        lax.rsqrt(jnp.mean(r.resid_two[...] * r.resid_two[...], axis=-1, keepdims=True) + norm_eps),
+        gain_three,
+    )
+    branch_two = low(grad_two)
+    narrow_grad = dot_tn(branch_two, r.act[...])
+    r.pre[...] = low(dot_nn(branch_two, narrow_w[...]) * r.slope[...])
+    widen_grad = dot_tn(r.pre[...], r.input_two[...])
+    resid_one = r.resid_one[...]
+    inverse_two = lax.rsqrt(jnp.mean(resid_one * resid_one, axis=-1, keepdims=True) + norm_eps)
+    from_two, gain_grad_two = rms_back(dot_nn(r.pre[...], widen_w[...]), resid_one, inverse_two, gain_two)
+    grad_one = grad_two + from_two
+    r.grad_one[...] = grad_one
+    branch_one = low(grad_one)
+    merge_grad = dot_tn(branch_one, r.attended[...])
+    r.mixed[...] = low(dot_nn(branch_one, merge_w[...]))
+
+    tail, head_pack = r.tail_pack, r.head_pack
+    for d in range(2 * chips):
+        at = (d % 2, d // 2 % 4, d // 8)
+        tail[*at, pl.ds(0, 32), :] = low(widen_grad[32 * d : 32 * d + 32])
+        tail[*at, pl.ds(32, 32), :] = low(
+            jnp.concatenate(
+                [
+                    narrow_grad[8 * d : 8 * d + 8, i * width : (i + 1) * width]
+                    for i in range(hidden // width)
+                ],
+                axis=0,
+            )
+        )
+    reduce_tail = Reduce(place, tail, r.tail_pair, r.tail_sum, r.tail_plane, r.tail_part, r.tail_line, r.tail_sems)
+    reduce_head = Reduce(place, head_pack, r.head_pair, r.head_sum, r.head_plane, r.head_part, r.head_line, r.head_sems)
+    reduce_tail.to_pair()
+    dq, dkv = r.dq, r.dkv
+    dq[...] = jnp.zeros_like(dq)
+    dkv[...] = jnp.zeros_like(dkv)
+
+    def attend_back(head):
+        mixed = of_head(r.mixed[...], head)
+        query = of_head(r.query[...], head)
+        own, other = prob[head, :, 0:tokens], prob[head, :, tokens : 2 * tokens]
+        own_grad = dot_nt(mixed, kv[0, :, width : 2 * width])
+        other_grad = dot_nt(mixed, kv[1, :, width : 2 * width])
+        inner = jnp.sum(own * own_grad, axis=-1, keepdims=True) + jnp.sum(
+            other * other_grad, axis=-1, keepdims=True
+        )
+        own_score = low(own * (own_grad - inner))
+        other_score = low(other * (other_grad - inner))
+        dq[...] += dot_nn(own_score, of_head(kv[0, :, 0:width], head)) + dot_nn(
+            other_score, of_head(kv[1, :, 0:width], head)
+        )
+        dkv[0, :, 0:width] += dot_tn(own_score, query)
+        dkv[1, :, 0:width] += dot_tn(other_score, query)
+        dkv[0, :, width : 2 * width] += dot_tn(low(own), mixed)
+        dkv[1, :, width : 2 * width] += dot_tn(low(other), mixed)
+
+    for head in range(HEADS):
+        attend_back(head)
+        if head % 2:
+            gather_u.advance(2)
+        if head == 3:
+            reduce_tail.to_plane()
+    back = r.back
+    back[0, :, 0:width] = low(dkv[1, :, 0:width] * scaling)
+    back[0, :, width : 2 * width] = low(dkv[1, :, width : 2 * width])
+    back_copy = remote(back.at[0], back.at[1], r.back_send, r.back_recv, chip, 1 - core)
+    back_copy.start()
+    back_copy.wait_recv()
+    qkv_grad = r.qkv_grad
+    qkv_grad[:, 0:width] = low(dq[...] * scaling)
+    qkv_grad[:, width : 2 * width] = low(dkv[0, :, 0:width] * scaling + wide(back[1, :, 0:width]))
+    qkv_grad[:, 2 * width : 3 * width] = low(dkv[0, :, width : 2 * width] + wide(back[1, :, width : 2 * width]))
+    qkv_wgrad = dot_tn(qkv_grad[...], r.input_one[...])
+    resid_zero = r.resid_zero[...]
+    inverse_one = lax.rsqrt(jnp.mean(resid_zero * resid_zero, axis=-1, keepdims=True) + norm_eps)
+    from_one, gain_grad_one = rms_back(dot_nn(qkv_grad[...], qkv_w[...]), resid_zero, inverse_one, gain_one)
+    resid_grad = r.grad_one[...] + from_one
+    r.resid_grad[...] = resid_grad
+    pos_grad = jnp.transpose(resid_grad)
+    nothing = jnp.zeros((8, width), jnp.float32)
+    for d in range(2 * chips):
+        at = (d % 2, d // 2 % 4, d // 8)
+        head_pack[*at, pl.ds(0, 32), :] = low(
+            jnp.concatenate([qkv_wgrad[24 * d : 24 * d + 24], merge_grad[8 * d : 8 * d + 8]], axis=0)
+        )
+        pos_piece = pos_grad[8 * d : 8 * d + 8]
+        head_pack[*at, pl.ds(32, 16), :] = low(
+            jnp.concatenate(
+                [jnp.where(core == 0, pos_piece, nothing), jnp.where(core == 0, nothing, pos_piece)], axis=0
+            )
+        )
+    reduce_head.to_pair()
+    gain_buf = r.gain_buf
+    gain_buf[chip] = jnp.concatenate([gain_grad_one, gain_grad_two, gain_grad_three], axis=1)
+    gain_there = Scatter(place, None, gain_buf, r.gain_send, r.gain_recv)
+    gain_there.start()
+    reduce_tail.to_line()
+    gather_u.advance(chips)
+    reduce_head.to_plane()
+    gather_u.arrived(0, other=True)
+    spread_norm.arrived()
+    cand_grad = r.acc
+    cand_grad[...] = jnp.zeros_like(cand_grad)
+    corr_col = r.corr_col[:, 0:1]
+    own_cand = cand_buf[me]
+    event_row = jnp.where(iota_of((1, both), 1) + 1 < own_length, 1.0 / total_events, 0.0)
+
+    def give_block(there, own):
+        block_rows = pair_rows(user_buf, there)
+        coef = jnp.exp((dot_nt(own_cand, block_rows) - corr_col) - pair_row(norm_buf, there))
+        if own:
+            coef = coef - jnp.where((chip_row == chip_col + 1) & (corr_col < 1e29), event_row, 0.0)
+        cand_grad[...] += dot_nn(low(coef), block_rows)
+
+    def grad_step(step, carry):
+        gather_u.arrived(step, other=True)
+        give_block(place.relative(step), False)
+        return carry
+
+    give_block(chip, True)
+    lax.fori_loop(1, chips // 2, grad_step, 0)
+    reduce_head.to_line()
+    lax.fori_loop(chips // 2, chips, grad_step, 0)
+
+    emb_grad = low(r.resid_grad[...] + cand_grad[...])
+    back_out, back_in = r.back_out, r.back_in
+    back_out[...] = low(dot_nn(r.spread[...], emb_grad)).reshape(chips, capacity, width)
+    back_in[core, chip] = back_out[chip]
+    rows_back = Scatter(place, back_out, back_in.at[core], r.rows_send, r.rows_recv)
+    rows_back.start()
+
+    shard = r.shard_grad
+    shard[0:64] = reduce_tail.total()
+    shard[64:112] = reduce_head.total()
+    total = shard[...]
+    gain_there.arrived()
+    gain_total = gain_buf[0]
+    for step in range(1, chips):
+        gain_total = gain_total + gain_buf[step]
+    gain_pair = r.gain_pair
+    gain_pair[core] = gain_total
+    gain_copy = remote(gain_pair.at[core], gain_pair.at[core], r.gp_send, r.gp_recv, chip, 1 - core)
+    gain_copy.start()
+    gain_copy.wait_recv()
+    gain_total = gain_pair[0] + gain_pair[1]
+    r.gain_grad[...] = gain_total
+    gain_lane = iota_of((1, 3 * width), 1)
+    gain_mine = lax.div(lax.rem(gain_lane, width), 8) == me
+    square = jnp.sum(total * total, axis=0, keepdims=True)
+    square = jnp.sum(square, axis=1, keepdims=True)
+    square = square + jnp.sum(jnp.where(gain_mine, gain_total * gain_total, 0.0), axis=1, keepdims=True)
+
+    rows_back.arrived()
+    rows_pair = remote(back_in.at[core], back_in.at[core], r.rp_send, r.rp_recv, chip, 1 - core)
+    rows_pair.start()
+    asked_copy.wait_recv()
+    asked_all = jnp.concatenate([r.asked[0], r.asked[1]], axis=1).astype(jnp.int32)
+    rows_pair.wait_recv()
+    table_grad = r.table_grad
+    part_rows = TABLE_PART if rows_dev % TABLE_PART == 0 else 8
+    incoming = back_in[...].reshape(2 * asked, width)
+    r.square[...] = jnp.zeros_like(r.square)
+
+    def table_part(index, carry):
+        first = pl.multiple_of(index * part_rows, 8)
+        hot = low(wide(iota_of((part_rows, 2 * asked), 0) + first == asked_all))
+        grads = dot_nn(hot, incoming)
+        table_grad[pl.ds(first, part_rows), :] = grads
+        r.square[...] += jnp.sum(grads * grads, axis=0, keepdims=True)
+        return carry
+
+    lax.fori_loop(0, rows_dev // part_rows, table_part, 0)
+    square = square + 0.5 * jnp.sum(r.square[...], axis=1, keepdims=True)
+
+    scalar_buf = r.scalar_buf
+    lane = iota_of((1, 128), 1)
+    scalar_buf[me] = jnp.where(lane == 0, square, jnp.where(lane == 1, loss_own, 0.0))
+    spread_sums.start()
+    gather_a.sent()
+    gather_b.sent()
+    gather_c.sent()
+    gather_u.sent()
+    rows_there.sent()
+    rows_back.sent()
+    gain_there.sent()
+    spread_corr.sent()
+    spread_norm.sent()
+    reduce_tail.sent()
+    reduce_head.sent()
+    for copy in (asked_copy, kv_copy, back_copy, gain_copy, rows_pair):
+        copy.wait_send()
+    spread_sums.arrived()
+    sums = scalar_buf[0]
+    for d in range(1, 2 * chips):
+        sums = sums + scalar_buf[d]
+    r.sums[...] = jnp.where(lane == 2, total_events, sums)
+    spread_sums.sent()
+
+
+TABLE_PART = 224
+CHUNKS = 4
+ENDS = dict(
+    ids=0, lengths=0, home=0, freq=0, table=0, pos=0, qkv=0, merge=0, widen=0, narrow=0, gains=0,
+    table_grad=1, shard_grad=1, gain_grad=1, sums=1,
+)
+
+
+def scratch_of(sizes):
+    (chips, rows_dev, seq_len, width, hidden, capacity, tokens, key_rows) = sizes
+    f32, b16 = jnp.float32, jnp.bfloat16
+    devices, levels = 2 * chips, chips // 4
+    dma = pltpu.SemaphoreType.DMA
+    lanes = -(-rows_dev // 128) * 128
+    if lanes == rows_dev:
+        lanes += 128
+    sends = Gather.sends(chips)
+    shapes = dict(
+        wa=pltpu.VMEM((devices, 48, width), b16),
+        wb=pltpu.VMEM((devices, 80, width), b16),
+        cand=pltpu.VMEM((devices, tokens, width), b16),
+        corr=pltpu.VMEM((devices, 1, tokens), f32),
+        logit=pltpu.VMEM((chips // CHUNKS, tokens, 2 * tokens), f32),
+        user=pltpu.VMEM((devices, tokens, width), b16),
+        low_table=pltpu.VMEM((lanes, width), b16),
+        keys=pltpu.VMEM((key_rows, 384), f32),
+        home_all=pltpu.VMEM((chips, tokens), f32),
+        row_out=pltpu.VMEM((chips, capacity, width), b16),
+        row_in=pltpu.VMEM((chips, capacity, width), b16),
+        asked=pltpu.VMEM((2, 1, chips * capacity), f32),
+        spread=pltpu.VMEM((chips * capacity, tokens), b16),
+        corr_col=pltpu.VMEM((tokens, 128), f32),
+        qkv_w=pltpu.VMEM((3 * width, width), b16),
+        pos_w=pltpu.VMEM((width, tokens), f32),
+        gain_w=pltpu.VMEM((width, 128), f32),
+        gain_rows=pltpu.VMEM((8, width), f32),
+        merge_w=pltpu.VMEM((width, width), b16),
+        widen_w=pltpu.VMEM((hidden, width), b16),
+        narrow_w=pltpu.VMEM((width, hidden), b16),
+        resid_zero=pltpu.VMEM((tokens, width), f32),
+        resid_one=pltpu.VMEM((tokens, width), f32),
+        resid_two=pltpu.VMEM((tokens, width), f32),
+        input_one=pltpu.VMEM((tokens, width), b16),
+        input_two=pltpu.VMEM((tokens, width), b16),
+        query=pltpu.VMEM((tokens, width), b16),
+        kv=pltpu.VMEM((2, tokens, 2 * width), b16),
+        prob=pltpu.VMEM((HEADS, tokens, 2 * tokens), f32),
+        acc=pltpu.VMEM((tokens, width), f32),
+        attended=pltpu.VMEM((tokens, width), b16),
+        act=pltpu.VMEM((tokens, hidden), b16),
+        slope=pltpu.VMEM((tokens, hidden), f32),
+        pre=pltpu.VMEM((tokens, hidden), b16),
+        peaks=pltpu.VMEM((tokens, 128), f32),
+        totals=pltpu.VMEM((tokens, 128), f32),
+        norm=pltpu.VMEM((devices, 1, tokens), f32),
+        grad_one=pltpu.VMEM((tokens, width), f32),
+        mixed=pltpu.VMEM((tokens, width), b16),
+        tail_pack=pltpu.VMEM((2, 4, levels, 64, width), b16),
+        tail_pair=pltpu.VMEM((4, levels, 64, width), b16),
+        tail_sum=pltpu.VMEM((4, levels, 64, width), b16),
+        tail_plane=pltpu.VMEM((4, levels, 64, width), b16),
+        tail_part=pltpu.VMEM((levels, 64, width), b16),
+        tail_line=pltpu.VMEM((levels, 64, width), b16),
+        tail_sems=dma((10 + 2 * levels,)),
+        head_pack=pltpu.VMEM((2, 4, levels, 48, width), b16),
+        head_pair=pltpu.VMEM((4, levels, 48, width), b16),
+        head_sum=pltpu.VMEM((4, levels, 48, width), b16),
+        head_plane=pltpu.VMEM((4, levels, 48, width), b16),
+        head_part=pltpu.VMEM((levels, 48, width), b16),
+        head_line=pltpu.VMEM((levels, 48, width), b16),
+        head_sems=dma((10 + 2 * levels,)),
+        dq=pltpu.VMEM((tokens, width), f32),
+        dkv=pltpu.VMEM((2, tokens, 2 * width), f32),
+        back=pltpu.VMEM((2, tokens, 2 * width), b16),
+        qkv_grad=pltpu.VMEM((tokens, 3 * width), b16),
+        resid_grad=pltpu.VMEM((tokens, width), f32),
+        gain_buf=pltpu.VMEM((chips, 1, 3 * width), f32),
+        gain_pair=pltpu.VMEM((2, 1, 3 * width), f32),
+        back_out=pltpu.VMEM((chips, capacity, width), b16),
+        back_in=pltpu.VMEM((2, chips, capacity, width), b16),
+        square=pltpu.VMEM((1, width), f32),
+        scalar_buf=pltpu.VMEM((devices, 1, 128), f32),
+        wa_send=dma((sends,)), wa_recv=dma((devices,)),
+        wb_send=dma((sends,)), wb_recv=dma((devices,)),
+        cand_send=dma((sends,)), cand_recv=dma((devices,)),
+        user_send=dma((sends,)), user_recv=dma((devices,)),
+        row_send=dma((chips,)), row_recv=dma((chips,)),
+        rows_send=dma((chips,)), rows_recv=dma((chips,)),
+        gain_send=dma((chips,)), gain_recv=dma((chips,)),
+        norm_send=dma((devices,)), norm_recv=dma((devices,)),
+        corr_send=dma((devices,)), corr_recv=dma((devices,)),
+        scalar_send=dma((devices,)), scalar_recv=dma((devices,)),
+        asked_send=dma, asked_recv=dma,
+        kv_send=dma, kv_recv=dma,
+        back_send=dma, back_recv=dma,
+        gp_send=dma, gp_recv=dma,
+        rp_send=dma, rp_recv=dma,
+    )
+    return shapes
+
+
+def adam(weight, first, second, grad, rate):
+    first = beta_one * first + (1.0 - beta_one) * grad
+    second = beta_two * second + (1.0 - beta_two) * grad * grad
+    fix_one = 1.0 - beta_one**STEP
+    fix_two = 1.0 - beta_two**STEP
+    update = first / fix_one / (jnp.sqrt(second / fix_two) + adam_eps) + decay_rate * weight
+    return weight - rate * update, first, second
+
+
+def update_kernel(width, *refs):
+    (table_grad, shard, gain_grad, sums), refs = refs[:4], refs[4:]
+    ins, outs = refs[:21], refs[21:]
+    square = sums[0:1, 0:1]
+    norm = jnp.sqrt(square)
+    factor = jnp.minimum(1.0, clip_limit / norm)
+
+    def update(index, grad, rate):
+        new = adam(*(ref[...] for ref in ins[3 * index : 3 * index + 3]), grad * factor, rate)
+        for ref, value in zip(outs[3 + 3 * index : 6 + 3 * index], new):
+            ref[...] = value
+
+    update(0, table_grad[...], learn_rate)
+
+    @pl.when(pl.program_id(0) == 0)
+    def _():
+        outs[0][...] = sums[0:1, 1:2]
+        outs[1][...] = sums[0:1, 2:3]
+        outs[2][...] = norm
+        update(1, jnp.concatenate([shard[96:104, :], shard[104:112, :]], axis=1), learn_rate)
+        update(2, shard[64:88, :], learn_rate)
+        update(3, shard[88:96, :], learn_rate)
+        update(4, shard[0:32, :], learn_rate)
+        update(5, jnp.concatenate([shard[32 + 8 * i : 40 + 8 * i, :] for i in range(4)], axis=1), learn_rate)
+        update(6, gain_grad[...], gain_rate)
+
+
+def fused_body(*args):
+    (item_ids, lengths, home_row, log_freq) = args[:4]
+    weights = args[4:]
+    item_table = weights[0]
+    rows_dev, width = item_table.shape
+    chips = lax.axis_size("dp")
+    seq_len = item_ids.shape[1]
+    tokens = seq_len // 2
+    hidden = weights[12].shape[1] * 2 * chips
+    capacity = 2 * tokens // chips
+    key_rows = -(-home_row.shape[0] // (128 * 128)) * 128
+    sizes = (chips, rows_dev, seq_len, width, hidden, capacity, tokens, key_rows)
+    me = lax.axis_index("dp") * 2 + lax.axis_index("sub")
+    dense = [w.T for w in weights[3:18]]
+    gains = weights[18]
+    gains_in = jnp.pad(gains.T, ((0, 0), (0, width - 3)))
+    shapes = scratch_of(sizes)
+    vmem = pl.BlockSpec(memory_space=pltpu.VMEM)
+    smem = pl.BlockSpec(memory_space=pltpu.SMEM)
+    f32 = jnp.float32
+    table_grad, shard, gain_grad, sums = pl.pallas_call(
+        functools.partial(step_kernel, sizes),
+        out_shape=[
+            jax.ShapeDtypeStruct((rows_dev, width), f32),
+            jax.ShapeDtypeStruct((112, width), f32),
+            jax.ShapeDtypeStruct((1, 3 * width), f32),
+            jax.ShapeDtypeStruct((1, 128), f32),
+        ],
+        in_specs=[vmem, smem] + [vmem] * 9,
+        out_specs=[vmem] * 4,
+        scratch_shapes=list(shapes.values()),
+        compiler_params=pltpu.CompilerParams(
+            collective_id=0, has_side_effects=True, vmem_limit_bytes=60 * 2**20
+        ),
+    )(
+        item_ids, lengths, home_row.reshape(-1, 128), log_freq.reshape(-1, 128), item_table,
+        dense[0], dense[3], dense[6], dense[9], dense[12], gains_in,
+    )
+    gain_own = lax.dynamic_slice_in_dim(gain_grad.reshape(3, width), me * 8, 8, 1)
+    part = TABLE_PART if rows_dev % TABLE_PART == 0 else 8
+    table_spec = pl.BlockSpec((part, width), lambda i: (i, 0))
+
+    def whole(x):
+        return pl.BlockSpec(x.shape, lambda i: (0,) * len(x.shape))
+
+    small = dense + [weights[18], weights[19], weights[20]]
+    one = jax.ShapeDtypeStruct((1, 1), f32)
+    outs = pl.pallas_call(
+        functools.partial(update_kernel, width),
+        grid=(rows_dev // part,),
+        out_shape=[one] * 3 + [jax.ShapeDtypeStruct(x.shape, f32) for x in list(weights[:3]) + small],
+        in_specs=[table_spec, whole(shard), whole(gain_own), whole(sums)] + [table_spec] * 3 + [whole(x) for x in small],
+        out_specs=[whole(one)] * 3 + [table_spec] * 3 + [whole(x) for x in small],
+    )(table_grad, shard, gain_own, sums, *weights[:3], *small)
+    outs = list(outs)
+    return tuple(
+        [x.reshape(()) for x in outs[:3]] + outs[3:6] + [x.T for x in outs[6:21]] + outs[21:]
+    )
+
+
 def solution(mesh):
     placed = (
         P(),
@@ -472,8 +1527,9 @@
         P(None, ("dp", "sub")),
         P(None, ("dp", "sub")),
     )
+    fits = mesh.shape["sub"] == 2 and mesh.shape["dp"] == 16
     return jax.shard_map(
-        body,
+        fused_body if fits else body,
         mesh=mesh,
         in_specs=placed,
         out_specs=(

time: 1290 us -> 132 us (0.10)
  waiting for transfers between devices: 717 us -> 0 us
  blocking collectives: 332 us -> 0 us
  Pallas kernels: 0 us -> 128 us
  local copies, waits for them, and re-layouts: 85.9 us -> 2.03 us
  other arithmetic: 54.2 us -> 0.69 us
  matrix products: 52.8 us -> 0 us
  between operations: 23.5 us -> 0.84 us
    reduce_scatter x7 -> x0, waiting for transfers between devices: 562 us -> none  [the longest x1 136 us: body(): lax.psum_scatter(pieces.reshape(tokens_dev * lax.axis_size(('dp', 'sub'))...]
    all_gather x8 -> x0, blocking collectives: 237 us -> none  [the longest x1 41.8 us: body(): lax.all_gather(norm_gains.astype(jnp.bfloat16), ('dp', 'sub'), axis=1, ti...]
    unnamed x11 -> x0, waiting for transfers between devices: 131 us -> none
    pallas_call x0 -> x2, Pallas kernels: none -> 128 us  [the longest x1 119 us: fused_body(): pl.pallas_call(functools.partial(step_kernel, sizes), out_shape=[jax.Shap...]
    gather x5 -> x0, local copies, waits for them, and re-layouts: 53.2 us -> none  [the longest x1 45.5 us: body(): correction = log_freq[all_items]]
    dot_general x24 -> x0, matrix products: 52.8 us -> none  [the longest x6 16.8 us: dot_left_t(): lax.dot_general(left_mat, right_mat, (((0,), (0,)), ((), ())), preferred_...]
    psum x1 -> x0, blocking collectives: 41.1 us -> none  [body(): loss_sum, square_sum = lax.psum((loss_local, square_part), ('dp', 'sub'))]
    unnamed x1 -> x0, blocking collectives: 39 us -> none
  transfers between devices with their start and end apart: 12 -> 0, of which waited for: 8 -> 0; matrix products, arithmetic and copies ran while one was open for 9% -> 0% of each run, Pallas kernels for 0% -> 0%
where the time goes in v1:
time: 132 us
  Pallas kernels  128 us (97%)
  local copies, waits for them, and re-layouts  2.03 us (2%)
    pallas_call x1, Pallas kernels, fused_body(): pl.pallas_call(functools.partial(step_kernel, sizes), out_shape=[jax.Shap...  119 us
    pallas_call x1, Pallas kernels, fused_body(): pl.pallas_call(functools.partial(update_kernel, width), grid=(rows_dev //...  9.56 us

profile of v1, /device:TPU:0, one launch (start us, length us, event | category | flops | bytes accessed | tf_op | source)
XLA Modules:
  0.0 131.8 jit_solution(2042714059528706569)
XLA Ops:
  0.7 0.8 copy.49
  1.4 0.6 pad.4.refs_10_
  2.0 118.7 %shard_map.424 = (f32[1568,256]{1,0:T(8,128)}, f32[112,256]{1,0:T(8,128)}, f32[1,768]{1,0:T(1,128)}, f32[1,128]{1,0:T(1,128)}) custom-call(s32[16,512]{1,0:T(8,128)} %refs_0_.1, s32[16]{0:T(128)} %refs_1_.1, s32[196,128]{1,0:T(8,128)} %bitcast.40, f32[196,128]{1,0:T(8,128)} %bitcast.41, f32[1568,256]{1,0:T(8,128)} %refs_4_.3, f32[8,512]{1,0:T(8,128)} %bitcast.44, ...), custom_call_target="tpu_custom_call" | custom-call | tf_op jit(solution)/shard_map/pallas_call | solution.py:1462
  120.7 0.7 reduce
  121.4 0.7 constant_dynamic-slice_fusion.refs_2_
  122.1 9.6 %shard_map.425 = (f32[1,1]{1,0:T(1,128)}, f32[1,1]{1,0:T(1,128)}, f32[1,1]{1,0:T(1,128)}, f32[1568,256]{1,0:T(8,128)}, f32[1568,256]{1,0:T(8,128)}, /*index=5*/f...) custom-call(f32[1568,256]{1,0:T(8,128)} %get-tuple-element.52.refs_0, ...), custom_call_target="tpu_custom_call" | custom-call | tf_op jit(solution)/shard_map/pallas_call | solution.py:1489
  (1 shorter events, 0.0 us)

commit v2 on v1

--- a/solution.py
+++ b/solution.py
@@ -492,14 +492,9 @@
 
 
 def arrival_order(levels):
-    above = range(1, levels)
-    return (
-        [(0, 0), (0, 1), (0, 2)]
-        + [(level, 0) for level in above]
-        + [(0, 3)]
-        + [(level, corner) for level in above for corner in (1, 2)]
-        + [(level, 3) for level in above]
-    )
+    if levels == 4:
+        return [(0, 0), (0, 1), (0, 2), (1, 0), (2, 0), (0, 3), (1, 1), (1, 2), (3, 0), (2, 1), (2, 2), (1, 3), (3, 1), (3, 2), (2, 3), (3, 3)]
+    return [(level, corner) for level in range(levels) for corner in range(4)]
 
 
 class Place:
@@ -509,8 +504,12 @@
         self.core = lax.axis_index("sub")
         self.level = lax.div(self.chip, 4)
         self.corner = lax.rem(self.chip, 4)
+        self.inner = (self.level == 1) | (self.level == 2)
         self.near_x = self.level * 4 + flip(self.corner, 1)
         self.near_y = self.level * 4 + flip(self.corner, 2)
+
+    def step(self, way):
+        return arrival_order(self.chips // 4).index(way)
 
     def way(self, step):
         order = arrival_order(self.chips // 4)
@@ -541,65 +540,60 @@
     def __init__(self, place, buf, send, recv):
         self.place, self.buf, self.send, self.recv = place, buf, send, recv
         self.levels = place.chips // 4
-        self.passed = 1
-
-    def copy(self, block, sem, chip, core):
+        order = [(0, 1), (1, 0), (2, 0), (1, 2), (3, 0), (2, 1)]
+        self.queue = [place.step(at) for at in order]
+        self.waiting = set(range(1, place.chips))
+
+    def copy(self, block, sem, chip):
         return remote(
-            self.buf.at[block], self.buf.at[block], self.send.at[sem], self.recv.at[block], chip, core
+            self.buf.at[block], self.buf.at[block], self.send.at[sem], self.recv.at[block], chip, self.place.core
         )
-
-    def block(self, step, other=False):
-        place = self.place
-        return place.relative(step) * 2 + (1 - place.core if other else place.core)
 
     def send_on(self, step, action):
         place = self.place
-        block = self.block(step)
-        action(self.copy(block, step * 3, place.chip, 1 - place.core))
-
-        def to_x():
-            action(self.copy(block, step * 3 + 1, place.near_x, place.core))
-
-        def to_y():
-            action(self.copy(block, step * 3 + 2, place.near_y, place.core))
-
+        block = place.relative(step)
         level, corner = place.way(step)
-        if corner == 0:
-            to_x()
-            to_y()
-        elif corner == 1 and level % 2 == 0:
-            to_y()
-        elif corner == 2 and level % 2 == 1:
-            to_x()
+        last = level == self.levels - 1
+        if corner == 0 or (corner == 2 and level % 2 == 1 and not last):
+            action(self.copy(block, step * 2, place.near_x))
+        if corner == 0 or (corner == 1 and level % 2 == 0 and not last):
+            action(self.copy(block, step * 2 + 1, place.near_y))
+        if corner == 0 and last:
+            action(self.copy(block, place.chips * 2, place.level * 4 + 3 - place.corner))
+        if corner == 0 and level == 2:
+            @pl.when(place.inner)
+            def _():
+                action(self.copy(block, place.chips * 2 + 4, flip(place.level, 1) * 4 + place.corner))
 
     def along_z(self, action):
         place = self.place
-        block = self.block(0)
-        for step in range(1, self.levels):
+        for step in (1, 3, 2):
             chip = flip(place.level, step) * 4 + place.corner
-            action(self.copy(block, place.chips * 3 + step - 1, chip, place.core))
+            copy = self.copy(place.chip, place.chips * 2 + step, chip)
+            if step == 3:
+                pl.when(place.inner)(lambda copy=copy: action(copy))
+            else:
+                action(copy)
 
     def start(self):
         self.along_z(lambda copy: copy.start())
         self.send_on(0, lambda copy: copy.start())
 
-    def arrived(self, step, other=False):
-        place = self.place
-        self.copy(self.block(step, other), 0, place.chip, 1 - place.core).wait_recv()
-
-    def pass_on(self, step):
-        self.arrived(step)
-        self.send_on(step, lambda copy: copy.start())
+    def need(self, steps):
+        for step in steps:
+            if step in self.waiting:
+                self.waiting.remove(step)
+                self.copy(self.place.relative(step), 0, self.place.chip).wait_recv()
+            if step in self.queue:
+                self.queue.remove(step)
+                self.send_on(step, lambda copy: copy.start())
 
     def advance(self, count):
-        for _ in range(min(count, self.place.chips - self.passed)):
-            self.pass_on(self.passed)
-            self.passed += 1
+        self.need(self.queue[:count])
 
     def complete(self):
-        self.advance(self.place.chips)
-        for step in range(self.place.chips):
-            self.arrived(step, other=True)
+        self.advance(len(self.queue))
+        self.need(sorted(self.waiting))
 
     def sent(self):
         self.along_z(lambda copy: copy.wait_send())
@@ -608,35 +602,31 @@
 
     @staticmethod
     def sends(chips):
-        return chips * 3 + chips // 4 - 1
-
-
-class Spread:
+        return chips * 2 + 8
+
+
+class ShortGather(Gather):
     def __init__(self, place, buf, send, recv):
-        self.place, self.buf, self.send, self.recv = place, buf, send, recv
-        self.me, self.count = place.chip * 2 + place.core, place.chips * 2
-
-    def copy(self, other, at):
-        return remote(
-            self.buf.at[at], self.buf.at[at], self.send.at[other], self.recv.at[at],
-            lax.div(other, 2), lax.rem(other, 2),
-        )
-
-    def each(self, action):
-        def step(index, carry):
-            action(lax.rem(self.me + index, self.count))
-            return carry
-
-        lax.fori_loop(1, self.count, step, 0)
-
-    def start(self):
-        self.each(lambda other: self.copy(other, self.me).start())
-
-    def arrived(self):
-        self.each(lambda other: self.copy(other, other).wait_recv())
-
-    def sent(self):
-        self.each(lambda other: self.copy(other, self.me).wait_send())
+        super().__init__(place, buf, send, recv)
+        self.queue = [place.step((level, 0)) for level in range(1, self.levels)]
+
+    def send_on(self, step, action):
+        place = self.place
+        block = place.relative(step)
+        if place.way(step)[1] == 0:
+            action(self.copy(block, step * 2, place.near_x))
+            action(self.copy(block, step * 2 + 1, place.near_y))
+            action(self.copy(block, place.chips * 2 + 4 + place.way(step)[0], place.level * 4 + 3 - place.corner))
+
+    def along_z(self, action):
+        place = self.place
+        for step in (1, 3, 2):
+            chip = flip(place.level, step) * 4 + place.corner
+            action(self.copy(place.chip, place.chips * 2 + step, chip))
+
+
+def to_sibling(place, src, dst, sems):
+    return remote(src, dst, sems.at[0], sems.at[1], place.chip, 1 - place.core)
 
 
 class Scatter:
@@ -787,31 +777,42 @@
     me = chip * 2 + core
     tokens = half_slots
     wa, wb, cand_buf, user_buf = r.wa, r.wb, r.cand, r.user
-    gather_a = Gather(place, wa, r.wa_send, r.wa_recv)
-    gather_b = Gather(place, wb, r.wb_send, r.wb_recv)
+    gather_a = ShortGather(place, wa.at[core], r.wa_send, r.wa_recv)
+    gather_b = ShortGather(place, wb.at[core], r.wb_send, r.wb_recv)
     gather_c = Gather(place, cand_buf, r.cand_send, r.cand_recv)
     gather_u = Gather(place, user_buf, r.user_send, r.user_recv)
-    spread_corr = Spread(place, r.corr, r.corr_send, r.corr_recv)
-    spread_norm = Spread(place, r.norm, r.norm_send, r.norm_recv)
-    spread_sums = Spread(place, r.scalar_buf, r.scalar_send, r.scalar_recv)
+    spread_corr = Scatter(place, None, r.corr, r.corr_send, r.corr_recv)
+    spread_norm = Scatter(place, None, r.norm, r.norm_send, r.norm_recv)
+    pair_a = to_sibling(place, wa.at[core], wa.at[core], r.wa_pair)
+    pair_b = to_sibling(place, wb.at[core], wb.at[core], r.wb_pair)
+    pair_emb = to_sibling(place, r.emb_pair.at[core], r.emb_pair.at[core], r.emb_sems)
+    pair_corr = to_sibling(place, r.corr_pair.at[core], r.corr_pair.at[core], r.corr_sems)
+    pair_user = to_sibling(place, r.user_pair.at[core], r.user_pair.at[core], r.user_sems)
+    pair_soft = to_sibling(place, r.soft_out, r.soft_in, r.soft_sems)
+    pair_cand = to_sibling(place, r.cand_out, r.cand_in, r.cand_sems)
+    spread_sums = Scatter(place, None, r.scalar_buf, r.scalar_send, r.scalar_recv)
+    pair_sums = to_sibling(place, r.scalar_pair.at[core], r.scalar_pair.at[core], r.sums_sems)
 
     barrier = pltpu.get_barrier_semaphore()
 
     def greet(index, carry):
-        other = lax.rem(me + index, 2 * chips)
-        pl.semaphore_signal(
-            barrier, inc=1, device_id=(lax.div(other, 2), lax.rem(other, 2)), device_id_type=MESH_ID
-        )
+        other = lax.rem(chip + index, chips)
+        pl.semaphore_signal(barrier, inc=1, device_id=(other, core), device_id_type=MESH_ID)
         return carry
 
-    lax.fori_loop(1, 2 * chips, greet, 0)
-
+    lax.fori_loop(1, chips, greet, 0)
+    pl.semaphore_signal(barrier, inc=1, device_id=(chip, 1 - core), device_id_type=MESH_ID)
+
+    turn = r.turn
+    turn[...] = jnp.zeros_like(turn)
+    turn[0:3, 0:8] = r.gains[...]
+    gains_t = jnp.concatenate([jnp.transpose(turn[...])[0:8, :], jnp.zeros((8, width - 128), jnp.float32)], axis=1)
     pos_t = r.pos[...]
-    wa[me] = low(
-        jnp.concatenate([r.qkv[...], r.gains[...], pos_t[:, :width], pos_t[:, width:]], axis=0)
+    wa[core, chip] = low(
+        jnp.concatenate([r.qkv[...], gains_t, pos_t[:, :width], pos_t[:, width:]], axis=0)
     )
     narrow_t = r.narrow[...]
-    wb[me] = low(
+    wb[core, chip] = low(
         jnp.concatenate(
             [r.merge[...], r.widen[...]]
             + [narrow_t[:, i * width : (i + 1) * width] for i in range(hidden // width)]
@@ -851,7 +852,7 @@
     home_all = jnp.concatenate(home_rows, axis=0)
     r.home_all[...] = home_all
 
-    pl.semaphore_wait(barrier, 2 * chips - 1)
+    pl.semaphore_wait(barrier, chips)
     gather_a.start()
 
     upper = low(wide(iota_of((tokens, tokens), 0) <= iota_of((tokens, tokens), 1)))
@@ -875,7 +876,6 @@
     r.row_in[chip] = r.row_out[chip]
     rows_there = Scatter(place, r.row_out, r.row_in, r.row_send, r.row_recv)
     rows_there.start()
-    gather_b.start()
     wanted_row = jnp.transpose(jnp.broadcast_to(wanted, (asked, 128)))[0:1, :]
     r.asked[core] = wanted_row
     asked_copy = remote(
@@ -906,8 +906,10 @@
     row_pos = core * tokens + iota_of((1, tokens), 1)
     is_cand = (row_pos >= 1) & (row_pos < own_length)
     own_corr = jnp.where(is_cand, fa + fb + fc, -big_negative)
-    r.corr[me] = own_corr
+    r.corr[chip] = own_corr
+    r.corr_pair[core] = own_corr
     spread_corr.start()
+    pair_corr.start()
 
     def turned(row):
         return jnp.transpose(jnp.broadcast_to(row, (128, tokens)))[:, 0:1]
@@ -922,17 +924,21 @@
     is_event = col_pos + 1 < own_length
 
     gather_a.advance(3)
+    gather_b.start()
     rows_there.arrived()
     embedded = low(dot_tn(r.spread[...], r.row_in[...].reshape(asked, width)))
-    cand_buf[me] = embedded
+    cand_buf[chip] = embedded
+    r.emb_pair[core] = embedded
     gather_c.start()
-    gather_a.advance(3)
+    pair_emb.start()
+    gather_a.complete()
+    pair_a.start()
     gather_b.advance(3)
-    gather_a.complete()
+    pair_a.wait_recv()
     qkv_w, pos_w, gain_w = r.qkv_w, r.pos_w, r.gain_w
 
     def unpack_a(index, carry):
-        one, two = wide(wa[2 * index]), wide(wa[2 * index + 1])
+        one, two = wide(wa[0, index]), wide(wa[1, index])
         qkv_w[pl.ds(pl.multiple_of(index * 48, 16), 48), :] = low(jnp.concatenate([one[0:24], two[0:24]], axis=0))
         gain_w[pl.ds(pl.multiple_of(index * 16, 16), 16), :] = jnp.concatenate([one[24:32], two[24:32]], axis=0)[:, 0:128]
         early = jnp.concatenate([one[32:40], two[32:40]], axis=0)
@@ -945,18 +951,16 @@
     r.gain_rows[...] = gain_rows
     gain_one, gain_two, gain_three = (r.gain_rows[i : i + 1, :] for i in range(3))
 
-    resid_zero = wide(cand_buf[me]) + jnp.transpose(pos_w[...])
+    resid_zero = wide(cand_buf[chip]) + jnp.transpose(pos_w[...])
     r.resid_zero[...] = resid_zero
     normed, _ = rms_apply(resid_zero, gain_one)
     r.input_one[...] = low(normed)
     qkv_own = low(dot_nt(r.input_one[...], qkv_w[...]))
-    r.query[...] = qkv_own[:, 0:width]
     kv = r.kv
     kv[0] = qkv_own[:, width : 3 * width]
     kv_copy = remote(kv.at[0], kv.at[1], r.kv_send, r.kv_recv, chip, 1 - core)
     kv_copy.start()
 
-    gather_b.advance(3)
     kv_copy.wait_recv()
 
     head_dim = width // HEADS
@@ -965,43 +969,56 @@
     other_bias = jnp.where(core == 0, big_negative, 0.0)
     head_lane = lax.div(iota_of((1, width), 1), head_dim)
     prob = r.prob
-    mixed_sum = r.acc
-    mixed_sum[...] = jnp.zeros_like(mixed_sum)
     zero_low = jnp.zeros((), jnp.bfloat16)
+    both = 2 * tokens
 
     def of_head(values, head):
         return jnp.where(head_lane == head, values, zero_low)
 
+    def rows_of(head, size=tokens):
+        return slice(head * size, (head + 1) * size)
+
+    def stack(to, values):
+        for head in range(HEADS):
+            to[rows_of(head), :] = of_head(values, head)
+
+    def stack_pair(to, pair, lanes):
+        for head in range(HEADS):
+            to[rows_of(2 * head), :] = of_head(pair[0, :, lanes], head)
+            to[rows_of(2 * head + 1), :] = of_head(pair[1, :, lanes], head)
+
+    stack(r.query_rows, qkv_own[:, 0:width])
+    stack_pair(r.value_rows, kv, slice(width, 2 * width))
+
     def attend(head):
-        query = of_head(r.query[...], head)
+        query = r.query_rows[rows_of(head), :]
         own = dot_nt(query, kv[0, :, 0:width]) * scaling
         own = jnp.where(causal, own, big_negative)
         other = dot_nt(query, kv[1, :, 0:width]) * scaling + other_bias
-        peak = jnp.maximum(
-            jnp.max(own, axis=-1, keepdims=True), jnp.max(other, axis=-1, keepdims=True)
-        )
+        peak = jnp.max(jnp.maximum(own, other), axis=-1, keepdims=True)
         own = jnp.exp(own - peak)
         other = jnp.exp(other - peak)
-        total = jnp.sum(own, axis=-1, keepdims=True) + jnp.sum(other, axis=-1, keepdims=True)
-        share = 1.0 / total
+        share = 1.0 / jnp.sum(own + other, axis=-1, keepdims=True)
         own = own * share
         other = other * share
         prob[head, :, 0:tokens] = own
-        prob[head, :, tokens : 2 * tokens] = other
-        mixed_sum[...] += dot_nn(low(own), of_head(kv[0, :, width : 2 * width], head)) + dot_nn(
-            low(other), of_head(kv[1, :, width : 2 * width], head)
-        )
+        prob[head, :, tokens:both] = other
+        own, other = low(own), low(other)
+        r.prob_own[rows_of(head), :] = own
+        r.prob_other[rows_of(head), :] = other
+        r.prob_lanes[:, rows_of(2 * head)] = own
+        r.prob_lanes[:, rows_of(2 * head + 1)] = other
 
     for head in range(HEADS):
         attend(head)
-        if head % 2:
-            gather_b.advance(2)
-            gather_c.advance(1)
     gather_b.complete()
+    pair_b.start()
+    gather_c.advance(2)
+    pair_b.wait_recv()
     merge_w, widen_w, narrow_w = r.merge_w, r.widen_w, r.narrow_w
 
     def unpack_b(index, carry):
-        one, two = wide(wb[2 * index]), wide(wb[2 * index + 1])
+        one, two = wide(wb[0, index]), wide(wb[1, index])
         at16 = pl.ds(pl.multiple_of(index * 16, 16), 16)
         merge_w[at16, :] = low(jnp.concatenate([one[0:8], two[0:8]], axis=0))
         widen_w[pl.ds(pl.multiple_of(index * 64, 16), 64), :] = low(jnp.concatenate([one[8:40], two[8:40]], axis=0))
@@ -1013,7 +1030,7 @@
         return carry
 
     lax.fori_loop(0, chips, unpack_b, 0)
-    r.attended[...] = low(mixed_sum[...])
+    r.attended[...] = low(dot_nn(r.prob_lanes[...], r.value_rows[...]))
     resid_one = r.resid_zero[...] + dot_nt(r.attended[...], merge_w[...])
     r.resid_one[...] = resid_one
     normed, _ = rms_apply(resid_one, gain_two)
@@ -1024,83 +1041,84 @@
         act, slope = gelu_both(dot_nt(r.input_two[...], widen_w[part, :]))
         r.act[:, part] = low(act)
         r.slope[:, part] = slope
-        gather_c.advance(1)
     r.resid_two[...] += dot_nt(r.act[...], narrow_w[...])
     normed, _ = rms_apply(r.resid_two[...], gain_three)
-    user_buf[me] = low(normed)
+    user_buf[chip] = low(normed)
+    r.user_pair[core] = user_buf[chip]
     gather_u.start()
-
-    users = user_buf[me]
+    pair_user.start()
+
     gather_c.advance(2)
-    gather_c.arrived(0, other=True)
     spread_corr.arrived()
-    shifted = jnp.concatenate([wide(cand_buf[me])[1:, :], wide(cand_buf[chip * 2 + 1, pl.ds(0, 16), :])[0:1, :]], axis=0)
-    target_corr = jnp.concatenate([corr_col[1:, :], r.corr[chip * 2 + 1][:, 0:1]], axis=0)
-    target_logit = jnp.sum(wide(users) * shifted, axis=-1, keepdims=True) - target_corr
+    pair_emb.wait_recv()
+    pair_corr.wait_recv()
+    shifted = jnp.concatenate([wide(cand_buf[chip])[1:, :], wide(r.emb_pair[1, pl.ds(0, 16), :])[0:1, :]], axis=0)
+    target_corr = jnp.concatenate([corr_col[1:, :], r.corr_pair[1][:, 0:1]], axis=0)
+    target_logit = jnp.sum(wide(user_buf[chip]) * shifted, axis=-1, keepdims=True) - target_corr
     target_logit = jnp.where(is_event, target_logit, 0.0)
+    pair_user.wait_recv()
+    users = r.user_pair[...].reshape(2 * tokens, width)
     logit_buf, peaks, totals, acc = r.logit, r.peaks, r.totals, r.acc
     totals[...] = jnp.zeros_like(totals)
     acc[...] = jnp.zeros_like(acc)
-    both = 2 * tokens
     group = chips // CHUNKS
-    chip_row = core * tokens + iota_of((tokens, both), 0)
-    chip_col = iota_of((tokens, both), 1)
-
-    def pair_rows(buf, there):
-        return buf[pl.ds(2 * there, 2)].reshape(both, width)
-
-    def pair_row(buf, there):
-        return jnp.concatenate([buf[2 * there], buf[2 * there + 1]], axis=1)
+    pair_row = iota_of((both, tokens), 0)
+    pair_col = core * tokens + iota_of((both, tokens), 1)
 
     def fold(values, how):
         parts = [values[:, i : i + 128] for i in range(0, values.shape[1], 128)]
         return functools.reduce(how, parts)
 
-    peak = jnp.full((tokens, 1), big_negative, jnp.float32)
+    peak = jnp.full((both, 1), big_negative, jnp.float32)
     for chunk in range(CHUNKS):
-        gather_c.advance(group * (chunk + 1) - gather_c.passed)
+        gather_c.advance(1)
+        gather_c.need(range(group * chunk, group * (chunk + 1)))
         peaks[...] = jnp.broadcast_to(peak, peaks.shape)
 
-        def logit_step(index, carry):
-            step = chunk * group + index
-
-            @pl.when(step > 0)
-            def _():
-                gather_c.arrived(step, other=True)
-
+        steps = range(chunk * group, (chunk + 1) * group)
+        for index, step in enumerate(steps):
             there = place.relative(step)
-            logits = dot_nt(users, pair_rows(cand_buf, there)) - pair_row(r.corr, there)
+            logits = dot_nt(users, cand_buf[there]) - r.corr[there]
             logit_buf[index] = logits
             peaks[...] = jnp.maximum(peaks[...], fold(logits, jnp.maximum))
-            return carry
-
-        lax.fori_loop(0, group, logit_step, 0)
         before, peak = peak, jnp.max(peaks[...], axis=-1, keepdims=True)
         scale = jnp.exp(before - peak)
         totals[...] *= scale
         acc[...] *= scale
         if chunk > 0:
-            gather_u.advance(2)
-
-        def expo_step(index, carry):
-            there = place.relative(chunk * group + index)
+            gather_u.advance(1)
+
+        for index, step in enumerate(steps):
             expo = jnp.exp(logit_buf[index] - peak)
             totals[...] += fold(expo, jnp.add)
-            if chunk == 0:
-                expo = jnp.where((chip_col == chip_row + 1) & (index == 0), 0.0, expo)
-            acc[...] += dot_nn(low(expo), pair_rows(cand_buf, there))
-            return carry
-
-        lax.fori_loop(0, group, expo_step, 0)
+            if step == 0:
+                expo = jnp.where(pair_col == pair_row + 1, 0.0, expo)
+            acc[...] += dot_nn(low(expo), cand_buf[place.relative(step)])
     total = jnp.sum(totals[...], axis=-1, keepdims=True)
+    peaks[...] = jnp.broadcast_to(peak, peaks.shape)
+    totals[...] = jnp.broadcast_to(total, totals.shape)
+    own_rows = pl.ds(pl.multiple_of(core * tokens, tokens), tokens)
+    other_rows = pl.ds(pl.multiple_of((1 - core) * tokens, tokens), tokens)
+    soft_out, soft_in = r.soft_out, r.soft_in
+    soft_out[:, 0:width] = acc[other_rows, :]
+    soft_out[:, width : width + 128] = peaks[other_rows, :]
+    soft_out[:, width + 128 : width + 256] = totals[other_rows, :]
+    pair_soft.start()
+    pair_soft.wait_recv()
+    own_peak, own_total = peaks[own_rows, :][:, 0:1], totals[own_rows, :][:, 0:1]
+    other_peak = soft_in[:, width : width + 1]
+    peak = jnp.maximum(own_peak, other_peak)
+    own_scale, other_scale = jnp.exp(own_peak - peak), jnp.exp(other_peak - peak)
+    total = own_total * own_scale + soft_in[:, width + 128 : width + 129] * other_scale
+    soft = acc[own_rows, :] * own_scale + soft_in[:, 0:width] * other_scale
     log_total = peak + jnp.log(total)
     loss_own = jnp.sum(jnp.where(is_event, log_total - target_logit, 0.0), axis=0, keepdims=True)
     weight = jnp.where(is_event, 1.0 / total_events, 0.0)
     target_coef = wide(low(weight * (jnp.exp(target_logit - log_total) - 1.0)))
-    user_grad = acc[...] * (weight / total) + target_coef * shifted
+    user_grad = soft * (weight / total) + target_coef * shifted
     shift_col = jnp.where(is_event, log_total + jnp.log(total_events), -big_negative)
     norm_buf = r.norm
-    norm_buf[me] = jnp.transpose(jnp.broadcast_to(shift_col, (tokens, 128)))[0:1, :]
+    norm_buf[chip] = jnp.transpose(jnp.broadcast_to(shift_col, (tokens, 128)))[0:1, :]
     spread_norm.start()
     grad_two, gain_grad_three = rms_back(
         user_grad, r.resid_two[...],
@@ -1136,45 +1154,44 @@
     reduce_tail = Reduce(place, tail, r.tail_pair, r.tail_sum, r.tail_plane, r.tail_part, r.tail_line, r.tail_sems)
     reduce_head = Reduce(place, head_pack, r.head_pair, r.head_sum, r.head_plane, r.head_part, r.head_line, r.head_sems)
     reduce_tail.to_pair()
-    dq, dkv = r.dq, r.dkv
-    dq[...] = jnp.zeros_like(dq)
-    dkv[...] = jnp.zeros_like(dkv)
+    gather_u.advance(1)
+    stack(r.mixed_rows, r.mixed[...])
+    stack_pair(r.key_rows, kv, slice(0, width))
 
     def attend_back(head):
-        mixed = of_head(r.mixed[...], head)
-        query = of_head(r.query[...], head)
-        own, other = prob[head, :, 0:tokens], prob[head, :, tokens : 2 * tokens]
+        mixed = r.mixed_rows[rows_of(head), :]
+        own, other = prob[head, :, 0:tokens], prob[head, :, tokens:both]
         own_grad = dot_nt(mixed, kv[0, :, width : 2 * width])
         other_grad = dot_nt(mixed, kv[1, :, width : 2 * width])
-        inner = jnp.sum(own * own_grad, axis=-1, keepdims=True) + jnp.sum(
-            other * other_grad, axis=-1, keepdims=True
-        )
+        inner = jnp.sum(own * own_grad + other * other_grad, axis=-1, keepdims=True)
         own_score = low(own * (own_grad - inner))
         other_score = low(other * (other_grad - inner))
-        dq[...] += dot_nn(own_score, of_head(kv[0, :, 0:width], head)) + dot_nn(
-            other_score, of_head(kv[1, :, 0:width], head)
-        )
-        dkv[0, :, 0:width] += dot_tn(own_score, query)
-        dkv[1, :, 0:width] += dot_tn(other_score, query)
-        dkv[0, :, width : 2 * width] += dot_tn(low(own), mixed)
-        dkv[1, :, width : 2 * width] += dot_tn(low(other), mixed)
+        r.score_own[rows_of(head), :] = own_score
+        r.score_other[rows_of(head), :] = other_score
+        r.score_lanes[:, rows_of(2 * head)] = own_score
+        r.score_lanes[:, rows_of(2 * head + 1)] = other_score
 
     for head in range(HEADS):
         attend_back(head)
-        if head % 2:
-            gather_u.advance(2)
+        if head == 1:
+            gather_u.advance(1)
         if head == 3:
             reduce_tail.to_plane()
+            gather_u.advance(1)
+        if head == 5:
+            gather_u.advance(1)
     back = r.back
-    back[0, :, 0:width] = low(dkv[1, :, 0:width] * scaling)
-    back[0, :, width : 2 * width] = low(dkv[1, :, width : 2 * width])
+    back[0, :, 0:width] = low(dot_tn(r.score_other[...], r.query_rows[...]) * scaling)
+    back[0, :, width : 2 * width] = low(dot_tn(r.prob_other[...], r.mixed_rows[...]))
     back_copy = remote(back.at[0], back.at[1], r.back_send, r.back_recv, chip, 1 - core)
     back_copy.start()
+    qkv_grad = r.qkv_grad
+    qkv_grad[:, 0:width] = low(dot_nn(r.score_lanes[...], r.key_rows[...]) * scaling)
+    key_own = dot_tn(r.score_own[...], r.query_rows[...]) * scaling
+    value_own = dot_tn(r.prob_own[...], r.mixed_rows[...])
     back_copy.wait_recv()
-    qkv_grad = r.qkv_grad
-    qkv_grad[:, 0:width] = low(dq[...] * scaling)
-    qkv_grad[:, width : 2 * width] = low(dkv[0, :, 0:width] * scaling + wide(back[1, :, 0:width]))
-    qkv_grad[:, 2 * width : 3 * width] = low(dkv[0, :, width : 2 * width] + wide(back[1, :, width : 2 * width]))
+    qkv_grad[:, width : 2 * width] = low(key_own + wide(back[1, :, 0:width]))
+    qkv_grad[:, 2 * width : 3 * width] = low(value_own + wide(back[1, :, width : 2 * width]))
     qkv_wgrad = dot_tn(qkv_grad[...], r.input_one[...])
     resid_zero = r.resid_zero[...]
     inverse_one = lax.rsqrt(jnp.mean(resid_zero * resid_zero, axis=-1, keepdims=True) + norm_eps)
@@ -1199,41 +1216,43 @@
     gain_buf[chip] = jnp.concatenate([gain_grad_one, gain_grad_two, gain_grad_three], axis=1)
     gain_there = Scatter(place, None, gain_buf, r.gain_send, r.gain_recv)
     gain_there.start()
-    reduce_tail.to_line()
-    gather_u.advance(chips)
-    reduce_head.to_plane()
-    gather_u.arrived(0, other=True)
+    gather_u.complete()
     spread_norm.arrived()
     cand_grad = r.acc
     cand_grad[...] = jnp.zeros_like(cand_grad)
-    corr_col = r.corr_col[:, 0:1]
-    own_cand = cand_buf[me]
-    event_row = jnp.where(iota_of((1, both), 1) + 1 < own_length, 1.0 / total_events, 0.0)
+    both_cand = r.emb_pair[...].reshape(both, width)
+    both_corr = jnp.concatenate([turned(r.corr_pair[0]), turned(r.corr_pair[1])], axis=0)
+    event_row = jnp.where(row_pos + 1 < own_length, 1.0 / total_events, 0.0)
 
     def give_block(there, own):
-        block_rows = pair_rows(user_buf, there)
-        coef = jnp.exp((dot_nt(own_cand, block_rows) - corr_col) - pair_row(norm_buf, there))
+        block_rows = user_buf[there]
+        coef = jnp.exp((dot_nt(both_cand, block_rows) - both_corr) - norm_buf[there])
         if own:
-            coef = coef - jnp.where((chip_row == chip_col + 1) & (corr_col < 1e29), event_row, 0.0)
+            coef = coef - jnp.where((pair_row == pair_col + 1) & (both_corr < 1e29), event_row, 0.0)
         cand_grad[...] += dot_nn(low(coef), block_rows)
 
-    def grad_step(step, carry):
-        gather_u.arrived(step, other=True)
-        give_block(place.relative(step), False)
-        return carry
-
-    give_block(chip, True)
-    lax.fori_loop(1, chips // 2, grad_step, 0)
-    reduce_head.to_line()
-    lax.fori_loop(chips // 2, chips, grad_step, 0)
-
-    emb_grad = low(r.resid_grad[...] + cand_grad[...])
+    for step in range(chips):
+        give_block(place.relative(step), step == 0)
+    r.cand_out[...] = cand_grad[other_rows, :]
+    pair_cand.start()
+    reduce_head.to_plane()
+    pair_cand.wait_recv()
+
+    emb_grad = low(r.resid_grad[...] + (cand_grad[own_rows, :] + r.cand_in[...]))
     back_out, back_in = r.back_out, r.back_in
     back_out[...] = low(dot_nn(r.spread[...], emb_grad)).reshape(chips, capacity, width)
     back_in[core, chip] = back_out[chip]
     rows_back = Scatter(place, back_out, back_in.at[core], r.rows_send, r.rows_recv)
     rows_back.start()
-
+    reduce_tail.to_line()
+    asked_copy.wait_recv()
+    asked_all = jnp.concatenate([r.asked[0], r.asked[1]], axis=1).astype(jnp.int32)
+    part_rows = TABLE_PART if rows_dev % TABLE_PART == 0 else 8
+    parts = [pl.ds(first, part_rows) for first in range(0, rows_dev, part_rows)]
+    for part in parts:
+        r.hot[part, :] = low(wide(iota_of((part_rows, 2 * asked), 0) + part.start == asked_all))
+
+    reduce_head.to_line()
     shard = r.shard_grad
     shard[0:64] = reduce_tail.total()
     shard[64:112] = reduce_head.total()
@@ -1248,7 +1267,9 @@
     gain_copy.start()
     gain_copy.wait_recv()
     gain_total = gain_pair[0] + gain_pair[1]
-    r.gain_grad[...] = gain_total
+    gain_three_rows = [gain_total[:, i * width : (i + 1) * width] for i in range(3)]
+    gain_w[:, 0:8] = jnp.transpose(jnp.concatenate(gain_three_rows + [jnp.zeros((5, width), jnp.float32)], axis=0))
+    r.gain_grad[...] = gain_w[pl.ds(pl.multiple_of(me * 8, 8), 8), :]
     gain_lane = iota_of((1, 3 * width), 1)
     gain_mine = lax.div(lax.rem(gain_lane, width), 8) == me
     square = jnp.sum(total * total, axis=0, keepdims=True)
@@ -1258,28 +1279,22 @@
     rows_back.arrived()
     rows_pair = remote(back_in.at[core], back_in.at[core], r.rp_send, r.rp_recv, chip, 1 - core)
     rows_pair.start()
-    asked_copy.wait_recv()
-    asked_all = jnp.concatenate([r.asked[0], r.asked[1]], axis=1).astype(jnp.int32)
     rows_pair.wait_recv()
     table_grad = r.table_grad
-    part_rows = TABLE_PART if rows_dev % TABLE_PART == 0 else 8
     incoming = back_in[...].reshape(2 * asked, width)
-    r.square[...] = jnp.zeros_like(r.square)
-
-    def table_part(index, carry):
-        first = pl.multiple_of(index * part_rows, 8)
-        hot = low(wide(iota_of((part_rows, 2 * asked), 0) + first == asked_all))
-        grads = dot_nn(hot, incoming)
-        table_grad[pl.ds(first, part_rows), :] = grads
-        r.square[...] += jnp.sum(grads * grads, axis=0, keepdims=True)
-        return carry
-
-    lax.fori_loop(0, rows_dev // part_rows, table_part, 0)
-    square = square + 0.5 * jnp.sum(r.square[...], axis=1, keepdims=True)
+    table_square = jnp.zeros((1, width), jnp.float32)
+    for part in parts:
+        grads = dot_nn(r.hot[part, :], incoming)
+        table_grad[part, :] = grads
+        table_square = table_square + jnp.sum(grads * grads, axis=0, keepdims=True)
+    square = square + 0.5 * jnp.sum(table_square, axis=1, keepdims=True)
 
     scalar_buf = r.scalar_buf
     lane = iota_of((1, 128), 1)
-    scalar_buf[me] = jnp.where(lane == 0, square, jnp.where(lane == 1, loss_own, 0.0))
+    r.scalar_pair[core] = jnp.where(lane == 0, square, jnp.where(lane == 1, loss_own, 0.0))
+    pair_sums.start()
+    pair_sums.wait_recv()
+    scalar_buf[chip] = r.scalar_pair[0] + r.scalar_pair[1]
     spread_sums.start()
     gather_a.sent()
     gather_b.sent()
@@ -1292,11 +1307,12 @@
     spread_norm.sent()
     reduce_tail.sent()
     reduce_head.sent()
-    for copy in (asked_copy, kv_copy, back_copy, gain_copy, rows_pair):
+    pairs = (pair_a, pair_b, pair_emb, pair_corr, pair_user, pair_soft, pair_cand, pair_sums)
+    for copy in (asked_copy, kv_copy, back_copy, gain_copy, rows_pair, *pairs):
         copy.wait_send()
     spread_sums.arrived()
     sums = scalar_buf[0]
-    for d in range(1, 2 * chips):
+    for d in range(1, chips):
         sums = sums + scalar_buf[d]
     r.sums[...] = jnp.where(lane == 2, total_events, sums)
     spread_sums.sent()
@@ -1320,12 +1336,21 @@
         lanes += 128
     sends = Gather.sends(chips)
     shapes = dict(
-        wa=pltpu.VMEM((devices, 48, width), b16),
-        wb=pltpu.VMEM((devices, 80, width), b16),
-        cand=pltpu.VMEM((devices, tokens, width), b16),
-        corr=pltpu.VMEM((devices, 1, tokens), f32),
-        logit=pltpu.VMEM((chips // CHUNKS, tokens, 2 * tokens), f32),
-        user=pltpu.VMEM((devices, tokens, width), b16),
+        wa=pltpu.VMEM((2, chips, 48, width), b16),
+        wb=pltpu.VMEM((2, chips, 80, width), b16),
+        cand=pltpu.VMEM((chips, tokens, width), b16),
+        corr=pltpu.VMEM((chips, 1, tokens), f32),
+        logit=pltpu.VMEM((chips // CHUNKS, 2 * tokens, tokens), f32),
+        user=pltpu.VMEM((chips, tokens, width), b16),
+        emb_pair=pltpu.VMEM((2, tokens, width), b16),
+        corr_pair=pltpu.VMEM((2, 1, tokens), f32),
+        user_pair=pltpu.VMEM((2, tokens, width), b16),
+        soft_out=pltpu.VMEM((tokens, width + 256), f32),
+        soft_in=pltpu.VMEM((tokens, width + 256), f32),
+        cand_out=pltpu.VMEM((tokens, width), f32),
+        cand_in=pltpu.VMEM((tokens, width), f32),
+        wa_pair=dma((2,)), wb_pair=dma((2,)), emb_sems=dma((2,)), corr_sems=dma((2,)),
+        user_sems=dma((2,)), soft_sems=dma((2,)), cand_sems=dma((2,)),
         low_table=pltpu.VMEM((lanes, width), b16),
         keys=pltpu.VMEM((key_rows, 384), f32),
         home_all=pltpu.VMEM((chips, tokens), f32),
@@ -1337,6 +1362,7 @@
         qkv_w=pltpu.VMEM((3 * width, width), b16),
         pos_w=pltpu.VMEM((width, tokens), f32),
         gain_w=pltpu.VMEM((width, 128), f32),
+        turn=pltpu.VMEM((128, 128), f32),
         gain_rows=pltpu.VMEM((8, width), f32),
         merge_w=pltpu.VMEM((width, width), b16),
         widen_w=pltpu.VMEM((hidden, width), b16),
@@ -1346,17 +1372,26 @@
         resid_two=pltpu.VMEM((tokens, width), f32),
         input_one=pltpu.VMEM((tokens, width), b16),
         input_two=pltpu.VMEM((tokens, width), b16),
-        query=pltpu.VMEM((tokens, width), b16),
+        query_rows=pltpu.VMEM((HEADS * tokens, width), b16),
+        mixed_rows=pltpu.VMEM((HEADS * tokens, width), b16),
+        key_rows=pltpu.VMEM((2 * HEADS * tokens, width), b16),
+        value_rows=pltpu.VMEM((2 * HEADS * tokens, width), b16),
+        prob_own=pltpu.VMEM((HEADS * tokens, tokens), b16),
+        prob_other=pltpu.VMEM((HEADS * tokens, tokens), b16),
+        prob_lanes=pltpu.VMEM((tokens, 2 * HEADS * tokens), b16),
+        score_own=pltpu.VMEM((HEADS * tokens, tokens), b16),
+        score_other=pltpu.VMEM((HEADS * tokens, tokens), b16),
+        score_lanes=pltpu.VMEM((tokens, 2 * HEADS * tokens), b16),
         kv=pltpu.VMEM((2, tokens, 2 * width), b16),
         prob=pltpu.VMEM((HEADS, tokens, 2 * tokens), f32),
-        acc=pltpu.VMEM((tokens, width), f32),
+        acc=pltpu.VMEM((2 * tokens, width), f32),
         attended=pltpu.VMEM((tokens, width), b16),
         act=pltpu.VMEM((tokens, hidden), b16),
         slope=pltpu.VMEM((tokens, hidden), f32),
         pre=pltpu.VMEM((tokens, hidden), b16),
-        peaks=pltpu.VMEM((tokens, 128), f32),
-        totals=pltpu.VMEM((tokens, 128), f32),
-        norm=pltpu.VMEM((devices, 1, tokens), f32),
+        peaks=pltpu.VMEM((2 * tokens, 128), f32),
+        totals=pltpu.VMEM((2 * tokens, 128), f32),
+        norm=pltpu.VMEM((chips, 1, tokens), f32),
         grad_one=pltpu.VMEM((tokens, width), f32),
         mixed=pltpu.VMEM((tokens, width), b16),
         tail_pack=pltpu.VMEM((2, 4, levels, 64, width), b16),
@@ -1373,8 +1408,6 @@
         head_part=pltpu.VMEM((levels, 48, width), b16),
         head_line=pltpu.VMEM((levels, 48, width), b16),
         head_sems=dma((10 + 2 * levels,)),
-        dq=pltpu.VMEM((tokens, width), f32),
-        dkv=pltpu.VMEM((2, tokens, 2 * width), f32),
         back=pltpu.VMEM((2, tokens, 2 * width), b16),
         qkv_grad=pltpu.VMEM((tokens, 3 * width), b16),
         resid_grad=pltpu.VMEM((tokens, width), f32),
@@ -1382,18 +1415,20 @@
         gain_pair=pltpu.VMEM((2, 1, 3 * width), f32),
         back_out=pltpu.VMEM((chips, capacity, width), b16),
         back_in=pltpu.VMEM((2, chips, capacity, width), b16),
-        square=pltpu.VMEM((1, width), f32),
-        scalar_buf=pltpu.VMEM((devices, 1, 128), f32),
-        wa_send=dma((sends,)), wa_recv=dma((devices,)),
-        wb_send=dma((sends,)), wb_recv=dma((devices,)),
-        cand_send=dma((sends,)), cand_recv=dma((devices,)),
-        user_send=dma((sends,)), user_recv=dma((devices,)),
+        hot=pltpu.VMEM((rows_dev, 2 * chips * capacity), b16),
+        scalar_buf=pltpu.VMEM((chips, 1, 128), f32),
+        scalar_pair=pltpu.VMEM((2, 1, 128), f32),
+        sums_sems=dma((2,)),
+        wa_send=dma((sends,)), wa_recv=dma((chips,)),
+        wb_send=dma((sends,)), wb_recv=dma((chips,)),
+        cand_send=dma((sends,)), cand_recv=dma((chips,)),
+        user_send=dma((sends,)), user_recv=dma((chips,)),
         row_send=dma((chips,)), row_recv=dma((chips,)),
         rows_send=dma((chips,)), rows_recv=dma((chips,)),
         gain_send=dma((chips,)), gain_recv=dma((chips,)),
-        norm_send=dma((devices,)), norm_recv=dma((devices,)),
-        corr_send=dma((devices,)), corr_recv=dma((devices,)),
-        scalar_send=dma((devices,)), scalar_recv=dma((devices,)),
+        norm_send=dma((chips,)), norm_recv=dma((chips,)),
+        corr_send=dma((chips,)), corr_recv=dma((chips,)),
+        scalar_send=dma((chips,)), scalar_recv=dma((chips,)),
         asked_send=dma, asked_recv=dma,
         kv_send=dma, kv_recv=dma,
         back_send=dma, back_recv=dma,
@@ -1412,9 +1447,9 @@
     return weight - rate * update, first, second
 
 
-def update_kernel(width, *refs):
+def update_kernel(*refs):
     (table_grad, shard, gain_grad, sums), refs = refs[:4], refs[4:]
-    ins, outs = refs[:21], refs[21:]
+    ins, outs, turn = refs[:21], refs[21:-1], refs[-1]
     square = sums[0:1, 0:1]
     norm = jnp.sqrt(square)
     factor = jnp.minimum(1.0, clip_limit / norm)
@@ -1436,7 +1471,8 @@
         update(3, shard[88:96, :], learn_rate)
         update(4, shard[0:32, :], learn_rate)
         update(5, jnp.concatenate([shard[32 + 8 * i : 40 + 8 * i, :] for i in range(4)], axis=1), learn_rate)
-        update(6, gain_grad[...], gain_rate)
+        turn[0:8, :] = gain_grad[...]
+        update(6, jnp.transpose(turn[...])[0:3, 0:8], gain_rate)
 
 
 def fused_body(*args):
@@ -1451,10 +1487,7 @@
     capacity = 2 * tokens // chips
     key_rows = -(-home_row.shape[0] // (128 * 128)) * 128
     sizes = (chips, rows_dev, seq_len, width, hidden, capacity, tokens, key_rows)
-    me = lax.axis_index("dp") * 2 + lax.axis_index("sub")
     dense = [w.T for w in weights[3:18]]
-    gains = weights[18]
-    gains_in = jnp.pad(gains.T, ((0, 0), (0, width - 3)))
     shapes = scratch_of(sizes)
     vmem = pl.BlockSpec(memory_space=pltpu.VMEM)
     smem = pl.BlockSpec(memory_space=pltpu.SMEM)
@@ -1464,7 +1497,7 @@
         out_shape=[
             jax.ShapeDtypeStruct((rows_dev, width), f32),
             jax.ShapeDtypeStruct((112, width), f32),
-            jax.ShapeDtypeStruct((1, 3 * width), f32),
+            jax.ShapeDtypeStruct((8, 128), f32),
             jax.ShapeDtypeStruct((1, 128), f32),
         ],
         in_specs=[vmem, smem] + [vmem] * 9,
@@ -1475,10 +1508,9 @@
         ),
     )(
         item_ids, lengths, home_row.reshape(-1, 128), log_freq.reshape(-1, 128), item_table,
-        dense[0], dense[3], dense[6], dense[9], dense[12], gains_in,
-    )
-    gain_own = lax.dynamic_slice_in_dim(gain_grad.reshape(3, width), me * 8, 8, 1)
-    part = TABLE_PART if rows_dev % TABLE_PART == 0 else 8
+        dense[0], dense[3], dense[6], dense[9], dense[12], weights[18],
+    )
+    part = rows_dev // 2 if rows_dev % 16 == 0 else rows_dev
     table_spec = pl.BlockSpec((part, width), lambda i: (i, 0))
 
     def whole(x):
@@ -1487,12 +1519,14 @@
     small = dense + [weights[18], weights[19], weights[20]]
     one = jax.ShapeDtypeStruct((1, 1), f32)
     outs = pl.pallas_call(
-        functools.partial(update_kernel, width),
+        update_kernel,
         grid=(rows_dev // part,),
         out_shape=[one] * 3 + [jax.ShapeDtypeStruct(x.shape, f32) for x in list(weights[:3]) + small],
-        in_specs=[table_spec, whole(shard), whole(gain_own), whole(sums)] + [table_spec] * 3 + [whole(x) for x in small],
+        in_specs=[table_spec, whole(shard), whole(gain_grad), whole(sums)] + [table_spec] * 3 + [whole(x) for x in small],
         out_specs=[whole(one)] * 3 + [table_spec] * 3 + [whole(x) for x in small],
-    )(table_grad, shard, gain_own, sums, *weights[:3], *small)
+        scratch_shapes=[pltpu.VMEM((128, 128), f32)],
+        compiler_params=pltpu.CompilerParams(vmem_limit_bytes=60 * 2**20),
+    )(table_grad, shard, gain_grad, sums, *weights[:3], *small)
     outs = list(outs)
     return tuple(
         [x.reshape(()) for x in outs[:3]] + outs[3:6] + [x.T for x in outs[6:21]] + outs[21:]

time: 132 us -> 115 us (0.87)
  Pallas kernels: 128 us -> 114 us
  local copies, waits for them, and re-layouts: 2.03 us -> 0 us
    pallas_call x1, Pallas kernels: 119 us -> 107 us  [fused_body(): pl.pallas_call(functools.partial(step_kernel, sizes), out_shape=[jax.Shap...]
    pallas_call x1, Pallas kernels: 9.56 us -> 7.17 us  [fused_body(): pl.pallas_call(update_kernel, grid=(rows_dev // part,), out_shape=[one] *...]
where the time goes in v2:
time: 115 us
  Pallas kernels  114 us (99%)
    pallas_call x1, Pallas kernels, fused_body(): pl.pallas_call(functools.partial(step_kernel, sizes), out_shape=[jax.Shap...  107 us
    pallas_call x1, Pallas kernels, fused_body(): pl.pallas_call(update_kernel, grid=(rows_dev // part,), out_shape=[one] *...  7.17 us

profile of v2, /device:TPU:0, one launch (start us, length us, event | category | flops | bytes accessed | tf_op | source)
XLA Modules:
  0.0 115.0 jit_solution(12639519745617847009)
XLA Ops:
  0.7 107.0 %shard_map.424 = (f32[1568,256]{1,0:T(8,128)}, f32[112,256]{1,0:T(8,128)}, f32[8,128]{1,0:T(8,128)}, f32[1,128]{1,0:T(1,128)}) custom-call(s32[16,512]{1,0:T(8,128)} %refs_0_.1, s32[16]{0:T(128)} %refs_1_.1, s32[196,128]{1,0:T(8,128)} %bitcast.39, f32[196,128]{1,0:T(8,128)} %bitcast.40, f32[1568,256]{1,0:T(8,128)} %refs_4_.3, f32[8,512]{1,0:T(8,128)} %bitcast.43, ...), custom_call_target="tpu_custom_call" | custom-call | tf_op jit(solution)/shard_map/pallas_call | solution.py:1495
  107.7 7.2 %shard_map.425 = (f32[1,1]{1,0:T(1,128)}, f32[1,1]{1,0:T(1,128)}, f32[1,1]{1,0:T(1,128)}, f32[1568,256]{1,0:T(8,128)}, f32[1568,256]{1,0:T(8,128)}, /*index=5*/f...) custom-call(f32[1568,256]{1,0:T(8,128)} %get-tuple-element.52.refs_0, ...), custom_call_target="tpu_custom_call" | custom-call | tf_op jit(solution)/shard_map/pallas_call | solution.py:1521

commit v3 on v2

--- a/solution.py
+++ b/solution.py
@@ -794,6 +794,8 @@
     pair_sums = to_sibling(place, r.scalar_pair.at[core], r.scalar_pair.at[core], r.sums_sems)
 
     barrier = pltpu.get_barrier_semaphore()
+    table_copy = pltpu.make_async_copy(r.table, r.table_here, r.table_sem)
+    table_copy.start()
 
     def greet(index, carry):
         other = lax.rem(chip + index, chips)
@@ -822,7 +824,6 @@
     )
 
     low_table = r.low_table
-    low_table[pl.ds(0, rows_dev), :] = low(r.table[...])
     pad_rows = low_table.shape[0] - rows_dev
     low_table[pl.ds(rows_dev, pad_rows), :] = jnp.zeros((pad_rows, width), jnp.bfloat16)
     keys = r.keys
@@ -870,6 +871,8 @@
     wanted = jnp.concatenate(wanted, axis=0)
     asked = chips * capacity
     lanes = low_table.shape[0]
+    table_copy.wait()
+    low_table[pl.ds(0, rows_dev), :] = low(r.table_here[...])
     hot_rows = low(wide(iota_of((asked, lanes), 1) == wanted.astype(jnp.int32)))
     out_rows = low(dot_nn(hot_rows, low_table[...])).reshape(chips, capacity, width)
     r.row_out[...] = out_rows
@@ -1009,6 +1012,7 @@
         r.prob_lanes[:, rows_of(2 * head)] = own
         r.prob_lanes[:, rows_of(2 * head + 1)] = other
 
+    gather_c.advance(1)
     for head in range(HEADS):
         attend(head)
     gather_b.complete()
@@ -1085,8 +1089,7 @@
         scale = jnp.exp(before - peak)
         totals[...] *= scale
         acc[...] *= scale
-        if chunk > 0:
-            gather_u.advance(1)
+        gather_u.advance((1, 2, 2, 1)[chunk])
 
         for index, step in enumerate(steps):
             expo = jnp.exp(logit_buf[index] - peak)
@@ -1275,6 +1278,9 @@
     square = jnp.sum(total * total, axis=0, keepdims=True)
     square = jnp.sum(square, axis=1, keepdims=True)
     square = square + jnp.sum(jnp.where(gain_mine, gain_total * gain_total, 0.0), axis=1, keepdims=True)
+    lane = iota_of((1, 128), 1)
+    r.scalar_pair[core] = jnp.where(lane == 0, square, jnp.where(lane == 1, loss_own, 0.0))
+    pair_sums.start()
 
     rows_back.arrived()
     rows_pair = remote(back_in.at[core], back_in.at[core], r.rp_send, r.rp_recv, chip, 1 - core)
@@ -1287,14 +1293,11 @@
         grads = dot_nn(r.hot[part, :], incoming)
         table_grad[part, :] = grads
         table_square = table_square + jnp.sum(grads * grads, axis=0, keepdims=True)
-    square = square + 0.5 * jnp.sum(table_square, axis=1, keepdims=True)
+    square = jnp.sum(table_square, axis=1, keepdims=True)
 
     scalar_buf = r.scalar_buf
-    lane = iota_of((1, 128), 1)
-    r.scalar_pair[core] = jnp.where(lane == 0, square, jnp.where(lane == 1, loss_own, 0.0))
-    pair_sums.start()
     pair_sums.wait_recv()
-    scalar_buf[chip] = r.scalar_pair[0] + r.scalar_pair[1]
+    scalar_buf[chip] = r.scalar_pair[0] + r.scalar_pair[1] + jnp.where(lane == 0, square, 0.0)
     spread_sums.start()
     gather_a.sent()
     gather_b.sent()
@@ -1336,6 +1339,8 @@
         lanes += 128
     sends = Gather.sends(chips)
     shapes = dict(
+        table_here=pltpu.VMEM((rows_dev, width), f32),
+        table_sem=dma,
         wa=pltpu.VMEM((2, chips, 48, width), b16),
         wb=pltpu.VMEM((2, chips, 80, width), b16),
         cand=pltpu.VMEM((chips, tokens, width), b16),
@@ -1500,7 +1505,7 @@
             jax.ShapeDtypeStruct((8, 128), f32),
             jax.ShapeDtypeStruct((1, 128), f32),
         ],
-        in_specs=[vmem, smem] + [vmem] * 9,
+        in_specs=[vmem, smem, vmem, vmem, pl.BlockSpec(memory_space=pl.ANY)] + [vmem] * 6,
         out_specs=[vmem] * 4,
         scratch_shapes=list(shapes.values()),
         compiler_params=pltpu.CompilerParams(

time: 115 us -> 106 us (0.922)
  Pallas kernels: 114 us -> 105 us
    pallas_call x1, Pallas kernels: 107 us -> 98 us  [fused_body(): pl.pallas_call(functools.partial(step_kernel, sizes), out_shape=[jax.Shap...]
where the time goes in v3:
time: 106 us
  Pallas kernels  105 us (99%)
    pallas_call x1, Pallas kernels, fused_body(): pl.pallas_call(functools.partial(step_kernel, sizes), out_shape=[jax.Shap...  98 us
    pallas_call x1, Pallas kernels, fused_body(): pl.pallas_call(update_kernel, grid=(rows_dev // part,), out_shape=[one] *...  7.17 us

profile of v3, /device:TPU:0, one launch (start us, length us, event | category | flops | bytes accessed | tf_op | source)
XLA Modules:
  0.0 106.0 jit_solution(10458830408431519712)
XLA Ops:
  0.7 98.0 %shard_map.424 = (f32[1568,256]{1,0:T(8,128)}, f32[112,256]{1,0:T(8,128)}, f32[8,128]{1,0:T(8,128)}, f32[1,128]{1,0:T(1,128)}) custom-call(s32[16,512]{1,0:T(8,128)} %refs_0_.1, s32[16]{0:T(128)} %refs_1_.1, s32[196,128]{1,0:T(8,128)} %bitcast.39, f32[196,128]{1,0:T(8,128)} %bitcast.40, f32[1568,256]{1,0:T(8,128)} %refs_4_.3, f32[8,512]{1,0:T(8,128)} %bitcast.43, ...), custom_call_target="tpu_custom_call" | custom-call | tf_op jit(solution)/shard_map/pallas_call | solution.py:1500
  98.7 7.2 %shard_map.425 = (f32[1,1]{1,0:T(1,128)}, f32[1,1]{1,0:T(1,128)}, f32[1,1]{1,0:T(1,128)}, f32[1568,256]{1,0:T(8,128)}, f32[1568,256]{1,0:T(8,128)}, /*index=5*/f...) custom-call(f32[1568,256]{1,0:T(8,128)} %get-tuple-element.52.refs_0, ...), custom_call_target="tpu_custom_call" | custom-call | tf_op jit(solution)/shard_map/pallas_call | solution.py:1526

commit v4 on v3

--- a/solution.py
+++ b/solution.py
@@ -651,7 +651,7 @@
             action(lax.rem(place.chip + index, place.chips))
             return carry
 
-        lax.fori_loop(1, place.chips, step, 0)
+        lax.fori_loop(1, place.chips, step, 0, unroll=True)
 
     def start(self):
         self.each(lambda chip: self.copy(chip, self.place.chip).start())
@@ -802,7 +802,7 @@
         pl.semaphore_signal(barrier, inc=1, device_id=(other, core), device_id_type=MESH_ID)
         return carry
 
-    lax.fori_loop(1, chips, greet, 0)
+    lax.fori_loop(1, chips, greet, 0, unroll=True)
     pl.semaphore_signal(barrier, inc=1, device_id=(chip, 1 - core), device_id_type=MESH_ID)
 
     turn = r.turn
@@ -1221,27 +1221,32 @@
     gain_there.start()
     gather_u.complete()
     spread_norm.arrived()
-    cand_grad = r.acc
-    cand_grad[...] = jnp.zeros_like(cand_grad)
-    both_cand = r.emb_pair[...].reshape(both, width)
     both_corr = jnp.concatenate([turned(r.corr_pair[0]), turned(r.corr_pair[1])], axis=0)
     event_row = jnp.where(row_pos + 1 < own_length, 1.0 / total_events, 0.0)
 
-    def give_block(there, own):
-        block_rows = user_buf[there]
-        coef = jnp.exp((dot_nt(both_cand, block_rows) - both_corr) - norm_buf[there])
-        if own:
-            coef = coef - jnp.where((pair_row == pair_col + 1) & (both_corr < 1e29), event_row, 0.0)
-        cand_grad[...] += dot_nn(low(coef), block_rows)
-
-    for step in range(chips):
-        give_block(place.relative(step), step == 0)
-    r.cand_out[...] = cand_grad[other_rows, :]
+    r.corr_both[...] = jnp.broadcast_to(both_corr, r.corr_both.shape)
+
+    def give_blocks(half, sums):
+        rows = r.emb_pair[half]
+        corr = r.corr_both[pl.ds(pl.multiple_of(half * tokens, tokens), tokens), :][:, 0:1]
+        row = half * tokens + iota_of((tokens, tokens), 0)
+        col = core * tokens + iota_of((tokens, tokens), 1)
+        for step in range(chips):
+            block_rows = user_buf[place.relative(step)]
+            coef = jnp.exp((dot_nt(rows, block_rows) - corr) - norm_buf[place.relative(step)])
+            if step == 0:
+                coef = coef - jnp.where((row == col + 1) & (corr < 1e29), event_row, 0.0)
+                sums[...] = dot_nn(low(coef), block_rows)
+            else:
+                sums[...] += dot_nn(low(coef), block_rows)
+
+    give_blocks(1 - core, r.cand_out)
     pair_cand.start()
+    give_blocks(core, r.cand_own)
     reduce_head.to_plane()
     pair_cand.wait_recv()
 
-    emb_grad = low(r.resid_grad[...] + (cand_grad[own_rows, :] + r.cand_in[...]))
+    emb_grad = low(r.resid_grad[...] + (r.cand_own[...] + r.cand_in[...]))
     back_out, back_in = r.back_out, r.back_in
     back_out[...] = low(dot_nn(r.spread[...], emb_grad)).reshape(chips, capacity, width)
     back_in[core, chip] = back_out[chip]
@@ -1354,6 +1359,8 @@
         soft_in=pltpu.VMEM((tokens, width + 256), f32),
         cand_out=pltpu.VMEM((tokens, width), f32),
         cand_in=pltpu.VMEM((tokens, width), f32),
+        cand_own=pltpu.VMEM((tokens, width), f32),
+        corr_both=pltpu.VMEM((2 * tokens, 128), f32),
         wa_pair=dma((2,)), wb_pair=dma((2,)), emb_sems=dma((2,)), corr_sems=dma((2,)),
         user_sems=dma((2,)), soft_sems=dma((2,)), cand_sems=dma((2,)),
         low_table=pltpu.VMEM((lanes, width), b16),

time: 106 us -> 106 us (level)
  no operation moved by 1% of the time
where the time goes in v4:
time: 106 us
  Pallas kernels  105 us (99%)
    pallas_call x1, Pallas kernels, fused_body(): pl.pallas_call(functools.partial(step_kernel, sizes), out_shape=[jax.Shap...  97.8 us
    pallas_call x1, Pallas kernels, fused_body(): pl.pallas_call(update_kernel, grid=(rows_dev // part,), out_shape=[one] *...  7.17 us

profile of v4, /device:TPU:0, one launch (start us, length us, event | category | flops | bytes accessed | tf_op | source)
XLA Modules:
  0.0 105.9 jit_solution(2323790734186297341)
XLA Ops:
  0.7 97.8 %shard_map.424 = (f32[1568,256]{1,0:T(8,128)}, f32[112,256]{1,0:T(8,128)}, f32[8,128]{1,0:T(8,128)}, f32[1,128]{1,0:T(1,128)}) custom-call(s32[16,512]{1,0:T(8,128)} %refs_0_.1, s32[16]{0:T(128)} %refs_1_.1, s32[196,128]{1,0:T(8,128)} %bitcast.39, f32[196,128]{1,0:T(8,128)} %bitcast.40, f32[1568,256]{1,0:T(8,128)} %refs_4_.3, f32[8,512]{1,0:T(8,128)} %bitcast.43, ...), custom_call_target="tpu_custom_call" | custom-call | tf_op jit(solution)/shard_map/pallas_call | solution.py:1507
  98.5 7.2 %shard_map.425 = (f32[1,1]{1,0:T(1,128)}, f32[1,1]{1,0:T(1,128)}, f32[1,1]{1,0:T(1,128)}, f32[1568,256]{1,0:T(8,128)}, f32[1568,256]{1,0:T(8,128)}, /*index=5*/f...) custom-call(f32[1568,256]{1,0:T(8,128)} %get-tuple-element.52.refs_0, ...), custom_call_target="tpu_custom_call" | custom-call | tf_op jit(solution)/shard_map/pallas_call | solution.py:1533
